TPU v7x, 512 devices: a whole 4x4x16 slice. The times are simulated.
512 devices in a mesh: rep: 4 (over z_hi), shard: 128 (over y, z_lo, x, core).
Axes of the slice: x: 4, y: 4, z: 16 (z_hi: 4, z_lo: 4; z = z_hi * 4 + z_lo), core: 2. Of those that a mesh axis runs over, the one named last changes fastest.
Arguments:
- grad_stack: bfloat16 [4, 4, 3, 4096, 1536], P('rep', None, None, 'shard'), may hold values from -6 to 6
- master_weight: float32 [4, 3, 4096, 1536], P(None, None, 'shard', 'rep'), may hold values from -0.046875 to 0.046875
- moment_one: float32 [4, 3, 4096, 1536], P(None, None, 'shard', 'rep'), may hold values from -0.18 to 0.18
- moment_two: float32 [4, 3, 4096, 1536], P(None, None, 'shard', 'rep'), may hold values from 0.02 to 0.2
- decode_rows: bfloat16 [2560, 4096], P('shard'), may hold values from -6 to 6
- norm_gain: bfloat16 [2, 4096], replicated, may hold values from 0.5 to 1.5
- route_ids: int32 [2, 2560, 2], P(None, 'shard'), may hold values from 0 to 3, all different within a row
- route_weights: float32 [2, 2560, 2], P(None, 'shard'), may hold values from 0.2 to 1
Outputs:
- new_moment_one: float32 [4, 3, 4096, 1536], P(None, None, 'shard', 'rep')
- new_moment_two: float32 [4, 3, 4096, 1536], P(None, None, 'shard', 'rep')
- branch_out: bfloat16 [2, 2560, 4096], P(None, 'shard', 'rep')
Inputs may be any that keep to these rules, and one draw needn't show every extreme that they name: `route_ids`: each row names 2 different experts, and every expert is named by some row.
All inputs are finite; a program needn't handle non-finite values.
Results may differ from a plain program's by a relative error of at most 0.029.
Values may be sent and summed in bfloat16 or wider, within the bound.
A program may use at most 64 MiB of HBM per device.

v0:
```python
import jax
import jax.numpy as jnp
from jax import lax
from jax.sharding import PartitionSpec as P

beta_one = 0.9
beta_two = 0.95
learn_rate = 0.05
adam_eps = 1e-08
bias_one = 1.0 - 0.9**10
bias_two = 1.0 - 0.95**10


def passed_along(x, axis, by):
    count = lax.axis_size(axis)
    return lax.ppermute(x, axis, [(i, (i + by) % count) for i in range(count)])


def route_share(chosen_ids, chosen_weights, expert_count):
    chosen = chosen_ids[:, :, None] == jnp.arange(expert_count, dtype=jnp.int32)[None, None, :]
    return jnp.sum(jnp.where(chosen, chosen_weights[:, :, None], 0.0), axis=1)


def expert_partial(full_rows, gain_row, weights_in, weights_out, expert_count):
    mean_sq = jnp.mean(full_rows.astype(jnp.float32) ** 2, axis=-1, keepdims=True)
    normed = (
        full_rows.astype(jnp.float32) * lax.rsqrt(mean_sq + 1e-06) * gain_row.astype(jnp.float32)
    ).astype(jnp.bfloat16)
    blocks = [normed]
    for ahead in range(1, expert_count):
        blocks.append(passed_along(normed, "shard", -ahead))
    stacked = jnp.concatenate(blocks, axis=0)
    row_total = stacked.shape[0]
    pieces = stacked.reshape(row_total, weights_in.shape[0], weights_in.shape[2])
    both = jnp.einsum("rnd,ngdf->rgf", pieces, weights_in, preferred_element_type=jnp.float32)
    hidden = (jax.nn.silu(both[:, 0]) * both[:, 1]).astype(jnp.bfloat16)
    partial_value = jnp.einsum(
        "rf,ndf->rnd", hidden, weights_out, preferred_element_type=jnp.float32
    )
    return partial_value.reshape(row_total, -1)


def expert_weight(shares, back):
    expert_count = shares.shape[1]
    wanted = (lax.axis_index("shard") - back) % expert_count
    picks = jnp.arange(expert_count, dtype=jnp.int32)[None, :] == wanted
    return jnp.sum(jnp.where(picks, shares, 0.0), axis=1, keepdims=True)


def return_cols(summed, shares, row_count):
    total = expert_weight(shares, 0) * summed[0:row_count]
    for back in range(1, shares.shape[1]):
        block = summed[back * row_count : (back + 1) * row_count]
        arrived = passed_along(block.astype(jnp.bfloat16), "shard", back).astype(block.dtype)
        total = total + expert_weight(shares, back) * arrived
    return total


def shards(
    grad_stack,
    master_weight,
    moment_one,
    moment_two,
    decode_rows,
    norm_gain,
    route_ids,
    route_weights,
):
    grad_total = lax.psum_scatter(
        grad_stack[0].astype(jnp.float32).astype(jnp.bfloat16),
        "rep",
        scatter_dimension=3,
        tiled=True,
    ).astype(jnp.float32)
    grad_mean = grad_total / lax.axis_size("rep")
    new_one = beta_one * moment_one + (1.0 - beta_one) * grad_mean
    new_two = beta_two * moment_two + (1.0 - beta_two) * grad_mean * grad_mean
    update = new_one / bias_one / (jnp.sqrt(new_two / bias_two) + adam_eps)
    local_served = (master_weight - learn_rate * update).astype(jnp.bfloat16)
    expert_count = local_served.shape[0]
    copies = lax.axis_size("shard") // expert_count
    outgoing = jnp.tile(local_served, (copies, 1, 1, 1))
    served = lax.all_to_all(outgoing, "shard", split_axis=0, concat_axis=0, tiled=True)
    weights_in = served[:, 0:2]
    weights_out = served[:, 2]
    row_count = decode_rows.shape[0]
    shares_first = route_share(route_ids[0], route_weights[0], expert_count)
    shares_second = route_share(route_ids[1], route_weights[1], expert_count)
    partial_value = expert_partial(decode_rows, norm_gain[0], weights_in, weights_out, expert_count)
    cols = lax.psum_scatter(
        partial_value.astype(jnp.bfloat16), "rep", scatter_dimension=1, tiled=True
    ).astype(jnp.float32)
    first_out = return_cols(cols, shares_first, row_count).astype(jnp.bfloat16)
    first_full = lax.all_gather(first_out, "rep", axis=1, tiled=True)
    middle = (decode_rows.astype(jnp.float32) + first_full.astype(jnp.float32)).astype(jnp.bfloat16)
    partial_two = expert_partial(middle, norm_gain[1], weights_in, weights_out, expert_count)
    cols_two = lax.psum_scatter(
        partial_two.astype(jnp.bfloat16), "rep", scatter_dimension=1, tiled=True
    ).astype(jnp.float32)
    second_out = return_cols(cols_two, shares_second, row_count).astype(jnp.bfloat16)
    return (new_one, new_two, jnp.stack([first_out, second_out]))


def solution(mesh):
    return jax.shard_map(
        shards,
        mesh=mesh,
        in_specs=(
            P("rep", None, None, "shard", None),
            P(None, None, "shard", "rep"),
            P(None, None, "shard", "rep"),
            P(None, None, "shard", "rep"),
            P("shard", None),
            P(),
            P(None, "shard", None),
            P(None, "shard", None),
        ),
        out_specs=(
            P(None, None, "shard", "rep"),
            P(None, None, "shard", "rep"),
            P(None, "shard", "rep"),
        ),
        check_vma=False,
    )
```

profile of v0, /device:TPU:1, one launch (start us, length us, event | category | flops | bytes accessed | tf_op | source)
XLA Modules:
  0.0 537.2 jit_solution(14897084275917141902)
XLA Ops:
  7.2 10.1 %copy.49 = bf16[4,3,32,1536]{2,1,0,3:T(4,128)(2,1)} copy(bf16[4,3,32,1536]{3,2,1,0:T(8,128)(2,1)} %bitcast.49) | data formatting | bytes 2359296
  17.3 11.2 %reshape.80 = bf16[1536,384]{1,0:T(8,128)(2,1)} reshape(bf16[1536,4,3,32]{3,2,1,0:T(4,128)(2,1)} %bitcast.45) | data formatting | bytes 2359296
  28.6 67.8 %reduce-scatter.10.cloned.1.call-done = bf16[384,384]{1,0:T(8,128)(2,1)} async-done(((bf16[1536,384]{1,0:T(8,128)(2,1)}), bf16[384,384]{1,0:T(8,128)(2,1)}) %reduce-scatter.10.cloned.1.call-update) | async-done | bytes 294928
  96.4 3.3 reshape.81
  99.7 1.2 copy.50
  100.9 2.5 subtract_convert_fusion
  103.4 5.1 tile.4
  108.5 12.9 %all-to-all-start = ((bf16[128,3,32,384]{3,2,1,0:T(8,128)(2,1)}), bf16[128,3,32,384]{3,2,1,0:T(8,128)(2,1)}, u32[]{:S(2)}, u32[]{:S(2)}) async-start(bf16[128,3,32,384]{3,2,1,0:T(8,128)(2,1)} %bitcast.42), calls=%async_computation | async-start | bytes 18874368 | tf_op jit(solution)/shard_map/all_to_all | solution.py:83
  121.8 10.3 %collective-permute-start.2 = (bf16[20,4096]{1,0:T(8,128)(2,1)S(1)}, bf16[20,4096]{1,0:T(8,128)(2,1)S(1)}, u32[]{:S(2)}, u32[]{:S(2)}) collective-permute-start(bf16[20,4096]{1,0:T(8,128)(2,1)S(1)} %fusion.20), channel_id=1, source_target_pairs={{0,125},{1,126},{2,127},{3,0},{4,1},{5,2},{6,3},{7,4},{8,5},{9,6},... | collective-permute-start | bytes 491528 | tf_op jit(solution)/shard_map/ppermute | solution.py:16
  132.1 2.5 collective-permute-start.1
  134.6 3.1 collective-permute-start
  137.7 138.6 %collective-permute-done.2 = bf16[20,4096]{1,0:T(8,128)(2,1)S(1)} collective-permute-done((bf16[20,4096]{1,0:T(8,128)(2,1)S(1)}, bf16[20,4096]{1,0:T(8,128)(2,1)S(1)}, u32[]{:S(2)}, u32[]{:S(2)}) %collective-permute-start.2) | collective-permute-done | bytes 163872 | tf_op jit(solution)/shard_map/ppermute | solution.py:16
  276.3 4.2 collective-permute-done.1
  280.7 0.6 copy.40
  281.3 1.0 copy.42
  282.3 49.4 %all-to-all-done = bf16[128,3,32,384]{3,2,1,0:T(8,128)(2,1)} async-done(((bf16[128,3,32,384]{3,2,1,0:T(8,128)(2,1)}), bf16[128,3,32,384]{3,2,1,0:T(8,128)(2,1)}, u32[]{:S(2)}, u32[]{:S(2)}) %all-to-all-start) | async-done | bytes 9437216 | tf_op jit(solution)/shard_map/all_to_all | solution.py:83
  331.8 3.6 slice.94
  335.4 6.9 %fusion.4 = f32[80,2,384]{2,0,1:T(8,128)S(1)} fusion(bf16[128,2,32,384]{3,2,1,0:T(8,128)(2,1)S(1)} %slice.94, bf16[80,128,32]{1,0,2:T(8,128)(2,1)S(1)} %copy.42), kind=kOutput, calls=%fused_computation.6 | convolution fusion | flops 503316480 | bytes 7192576 | tf_op jit(solution)/shard_map/rnd,ngdf->rgf/dot_general | solution.py:35
  342.3 2.2 slice.97
  344.5 1.9 convolution_convert_fusion.1
  346.7 50.5 %reduce-scatter.6.cloned.1.call-done = bf16[80,1024]{1,0:T(8,128)(2,1)} async-done(((bf16[80,4096]{1,0:T(8,128)(2,1)}), bf16[80,1024]{1,0:T(8,128)(2,1)}) %reduce-scatter.6.cloned.1.call-update) | async-done | bytes 163856 | tf_op jit(solution)/shard_map/reduce_scatter | solution.py:90
  397.1 0.9 fusion.34
  398.0 5.3 collective-permute-start.5
  403.4 3.0 collective-permute-start.4
  406.4 1.9 collective-permute-start.3
  408.4 1.4 collective-permute-done.5
  409.8 4.5 collective-permute-done.4
  414.2 0.9 add_convert_fusion.1
  415.1 16.2 %all_gather.3 = bf16[20,4096]{1,0:T(8,128)(2,1)S(1)} all-gather(bf16[20,1024]{1,0:T(8,128)(2,1)S(1)} %add_convert_fusion.1), channel_id=1, replica_groups=mesh['rep'=4,'shard'=128] {'rep'}, dimensions={1}, use_global_device_ids=true | all-gather | bytes 204800 | tf_op jit(solution)/shard_map/all_gather | solution.py:94
  431.6 6.1 %collective-permute-start.8 = (bf16[20,4096]{1,0:T(8,128)(2,1)S(1)}, bf16[20,4096]{1,0:T(8,128)(2,1)S(1)}, u32[]{:S(2)}, u32[]{:S(2)}) collective-permute-start(bf16[20,4096]{1,0:T(8,128)(2,1)S(1)} %fusion.17), channel_id=1, source_target_pairs={{0,125},{1,126},{2,127},{3,0},{4,1},{5,2},{6,3},{7,4},{8,5},{9,6},... | collective-permute-start | bytes 491528 | tf_op jit(solution)/shard_map/ppermute | solution.py:16
  437.7 2.8 collective-permute-start.7
  440.5 2.1 collective-permute-start.6
  442.7 4.3 collective-permute-done.7
  447.0 2.3 collective-permute-done.6
  449.3 1.0 pad_maximum_fusion.1
  450.3 2.2 copy.44
  452.5 2.6 copy.45
  455.1 9.9 %fusion.7 = f32[80,2,384]{2,0,1:T(8,128)S(1)} fusion(bf16[128,2,32,384]{3,2,1,0:T(8,128)(2,1)} %copy-done, bf16[80,128,32]{1,0,2:T(8,128)(2,1)} %copy.45), kind=kOutput, calls=%fused_computation.7 | convolution fusion | flops 503316480 | bytes 7192576 | tf_op jit(solution)/shard_map/rnd,ngdf->rgf/dot_general | solution.py:35
  465.0 1.9 convolution_convert_fusion
  466.9 44.5 %reduce-scatter.8.cloned.1.call-done = bf16[80,1024]{1,0:T(8,128)(2,1)} async-done(((bf16[80,4096]{1,0:T(8,128)(2,1)}), bf16[80,1024]{1,0:T(8,128)(2,1)}) %reduce-scatter.8.cloned.1.call-update) | async-done | bytes 163856 | tf_op jit(solution)/shard_map/reduce_scatter | solution.py:97
  511.5 0.9 fusion.33
  512.4 5.8 %collective-permute-start.11 = (bf16[20,1024]{1,0:T(8,128)(2,1)S(1)}, bf16[20,1024]{1,0:T(8,128)(2,1)S(1)}, u32[]{:S(2)}, u32[]{:S(2)}) collective-permute-start(bf16[20,1024]{1,0:T(8,128)(2,1)S(1)} %get-tuple-element.31), channel_id=1, source_target_pairs={{0,3},{1,4},{2,5},{3,6},{4,7},{5,8},{6,9},{7,10},{8,11},{9,12},{10... | collective-permute-start | bytes 122888 | tf_op jit(solution)/shard_map/ppermute | solution.py:16
  518.2 1.9 collective-permute-start.10
  520.1 2.1 collective-permute-start.9
  522.2 2.0 collective-permute-done.11
  524.2 4.8 collective-permute-done.10
  529.0 0.9 fusion.28
  529.9 0.7 copy.46
  (39 shorter events, 1.1 us)
Async XLA Ops:
  7.2 89.2 %reduce-scatter.10.cloned.1.call-start = ((), (), s32[]{:S(2)}) async-start(), calls=%async_computation.6 | async-start | bytes 1474560
  28.5 72.3 %copy-start.2 = (f32[4,3,32,384]{3,2,1,0:T(8,128)S(1)}, f32[4,3,32,384]{3,2,1,0:T(8,128)}, u32[]{:S(2)}) copy-start(f32[4,3,32,384]{3,2,1,0:T(8,128)} %param.9) | copy-start | bytes 1769476
  28.5 72.4 %copy-start.3 = (f32[4,3,32,384]{3,2,1,0:T(8,128)S(1)}, f32[4,3,32,384]{3,2,1,0:T(8,128)}, u32[]{:S(2)}) copy-start(f32[4,3,32,384]{3,2,1,0:T(8,128)} %param.11) | copy-start | bytes 1769476
  108.5 12.9 %copy-start.1 = (bf16[20,4096]{1,0:T(8,128)(2,1)S(1)}, bf16[20,4096]{1,0:T(8,128)(2,1)}, u32[]{:S(2)}) copy-start(bf16[20,4096]{1,0:T(8,128)(2,1)} %param.12) | copy-start | bytes 491524
  108.5 13.1 %copy-start.4 = (bf16[2,4096]{1,0:T(2,128)(2,1)S(1)}, bf16[2,4096]{1,0:T(2,128)(2,1)}, u32[]{:S(2)}) copy-start(bf16[2,4096]{1,0:T(2,128)(2,1)} %param.13) | copy-start | bytes 49156
  108.5 223.2 %all-to-all-start = ((bf16[128,3,32,384]{3,2,1,0:T(8,128)(2,1)}), bf16[128,3,32,384]{3,2,1,0:T(8,128)(2,1)}, u32[]{:S(2)}, u32[]{:S(2)}) async-start(bf16[128,3,32,384]{3,2,1,0:T(8,128)(2,1)} %bitcast.42), calls=%async_computation | async-start | bytes 18874368 | tf_op jit(solution)/shard_map/all_to_all | solution.py:83
  121.4 275.7 %reduce-scatter.6.cloned.1.call-start = ((), (), s32[]{:S(2)}) async-start(), calls=%async_computation.4 | async-start | bytes 819200 | tf_op jit(solution)/shard_map/reduce_scatter | solution.py:90
  121.8 154.5 %collective-permute-start.2 = (bf16[20,4096]{1,0:T(8,128)(2,1)S(1)}, bf16[20,4096]{1,0:T(8,128)(2,1)S(1)}, u32[]{:S(2)}, u32[]{:S(2)}) collective-permute-start(bf16[20,4096]{1,0:T(8,128)(2,1)S(1)} %fusion.20), channel_id=1, source_target_pairs={{0,125},{1,126},{2,127},{3,0},{4,1},{5,2},{6,3},{7,4},{8,5},{9,6},... | collective-permute-start | bytes 491528 | tf_op jit(solution)/shard_map/ppermute | solution.py:16
  132.1 148.4 %collective-permute-start.1 = (bf16[20,4096]{1,0:T(8,128)(2,1)S(1)}, bf16[20,4096]{1,0:T(8,128)(2,1)S(1)}, u32[]{:S(2)}, u32[]{:S(2)}) collective-permute-start(bf16[20,4096]{1,0:T(8,128)(2,1)S(1)} %fusion.20), channel_id=1, source_target_pairs={{0,126},{1,127},{2,0},{3,1},{4,2},{5,3},{6,4},{7,5},{8,6},{9,7},{1... | collective-permute-start | bytes 491528 | tf_op jit(solution)/shard_map/ppermute | solution.py:16
  134.6 145.9 %collective-permute-start = (bf16[20,4096]{1,0:T(8,128)(2,1)S(1)}, bf16[20,4096]{1,0:T(8,128)(2,1)S(1)}, u32[]{:S(2)}, u32[]{:S(2)}) collective-permute-start(bf16[20,4096]{1,0:T(8,128)(2,1)S(1)} %fusion.20), channel_id=1, source_target_pairs={{0,127},{1,0},{2,1},{3,2},{4,3},{5,4},{6,5},{7,6},{8,7},{9,8},{10,... | collective-permute-start | bytes 491528 | tf_op jit(solution)/shard_map/ppermute | solution.py:16
  335.4 6.9 %copy-start = (bf16[128,2,32,384]{3,2,1,0:T(8,128)(2,1)}, bf16[128,2,32,384]{3,2,1,0:T(8,128)(2,1)S(1)}, u32[]{:S(2)}) copy-start(bf16[128,2,32,384]{3,2,1,0:T(8,128)(2,1)S(1)} %slice.94) | copy-start | bytes 18874372
  344.5 2.1 copy-start.5
  344.5 2.1 copy-start.6
  346.5 165.0 %reduce-scatter.8.cloned.1.call-start = ((), (), s32[]{:S(2)}) async-start(), calls=%async_computation.5 | async-start | bytes 819200 | tf_op jit(solution)/shard_map/reduce_scatter | solution.py:97
  398.0 11.7 %collective-permute-start.5 = (bf16[20,1024]{1,0:T(8,128)(2,1)S(1)}, bf16[20,1024]{1,0:T(8,128)(2,1)S(1)}, u32[]{:S(2)}, u32[]{:S(2)}) collective-permute-start(bf16[20,1024]{1,0:T(8,128)(2,1)S(1)} %get-tuple-element.34), channel_id=1, source_target_pairs={{0,3},{1,4},{2,5},{3,6},{4,7},{5,8},{6,9},{7,10},{8,11},{9,12},{10... | collective-permute-start | bytes 122888 | tf_op jit(solution)/shard_map/ppermute | solution.py:16
  403.4 10.9 %collective-permute-start.4 = (bf16[20,1024]{1,0:T(8,128)(2,1)S(1)}, bf16[20,1024]{1,0:T(8,128)(2,1)S(1)}, u32[]{:S(2)}, u32[]{:S(2)}) collective-permute-start(bf16[20,1024]{1,0:T(8,128)(2,1)S(1)} %get-tuple-element.35), channel_id=1, source_target_pairs={{0,2},{1,3},{2,4},{3,5},{4,6},{5,7},{6,8},{7,9},{8,10},{9,11},{10,... | collective-permute-start | bytes 122888 | tf_op jit(solution)/shard_map/ppermute | solution.py:16
  406.4 7.9 %collective-permute-start.3 = (bf16[20,1024]{1,0:T(8,128)(2,1)S(1)}, bf16[20,1024]{1,0:T(8,128)(2,1)S(1)}, u32[]{:S(2)}, u32[]{:S(2)}) collective-permute-start(bf16[20,1024]{1,0:T(8,128)(2,1)S(1)} %get-tuple-element.33), channel_id=1, source_target_pairs={{0,1},{1,2},{2,3},{3,4},{4,5},{5,6},{6,7},{7,8},{8,9},{9,10},{10,1... | collective-permute-start | bytes 122888 | tf_op jit(solution)/shard_map/ppermute | solution.py:16
  431.6 11.1 %collective-permute-start.8 = (bf16[20,4096]{1,0:T(8,128)(2,1)S(1)}, bf16[20,4096]{1,0:T(8,128)(2,1)S(1)}, u32[]{:S(2)}, u32[]{:S(2)}) collective-permute-start(bf16[20,4096]{1,0:T(8,128)(2,1)S(1)} %fusion.17), channel_id=1, source_target_pairs={{0,125},{1,126},{2,127},{3,0},{4,1},{5,2},{6,3},{7,4},{8,5},{9,6},... | collective-permute-start | bytes 491528 | tf_op jit(solution)/shard_map/ppermute | solution.py:16
  437.7 9.3 %collective-permute-start.7 = (bf16[20,4096]{1,0:T(8,128)(2,1)S(1)}, bf16[20,4096]{1,0:T(8,128)(2,1)S(1)}, u32[]{:S(2)}, u32[]{:S(2)}) collective-permute-start(bf16[20,4096]{1,0:T(8,128)(2,1)S(1)} %fusion.17), channel_id=1, source_target_pairs={{0,126},{1,127},{2,0},{3,1},{4,2},{5,3},{6,4},{7,5},{8,6},{9,7},{1... | collective-permute-start | bytes 491528 | tf_op jit(solution)/shard_map/ppermute | solution.py:16
  440.5 8.7 %collective-permute-start.6 = (bf16[20,4096]{1,0:T(8,128)(2,1)S(1)}, bf16[20,4096]{1,0:T(8,128)(2,1)S(1)}, u32[]{:S(2)}, u32[]{:S(2)}) collective-permute-start(bf16[20,4096]{1,0:T(8,128)(2,1)S(1)} %fusion.17), channel_id=1, source_target_pairs={{0,127},{1,0},{2,1},{3,2},{4,3},{5,4},{6,5},{7,6},{8,7},{9,8},{10,... | collective-permute-start | bytes 491528 | tf_op jit(solution)/shard_map/ppermute | solution.py:16
  512.4 11.8 %collective-permute-start.11 = (bf16[20,1024]{1,0:T(8,128)(2,1)S(1)}, bf16[20,1024]{1,0:T(8,128)(2,1)S(1)}, u32[]{:S(2)}, u32[]{:S(2)}) collective-permute-start(bf16[20,1024]{1,0:T(8,128)(2,1)S(1)} %get-tuple-element.31), channel_id=1, source_target_pairs={{0,3},{1,4},{2,5},{3,6},{4,7},{5,8},{6,9},{7,10},{8,11},{9,12},{10... | collective-permute-start | bytes 122888 | tf_op jit(solution)/shard_map/ppermute | solution.py:16
  518.2 10.9 %collective-permute-start.10 = (bf16[20,1024]{1,0:T(8,128)(2,1)S(1)}, bf16[20,1024]{1,0:T(8,128)(2,1)S(1)}, u32[]{:S(2)}, u32[]{:S(2)}) collective-permute-start(bf16[20,1024]{1,0:T(8,128)(2,1)S(1)} %get-tuple-element.32), channel_id=1, source_target_pairs={{0,2},{1,3},{2,4},{3,5},{4,6},{5,7},{6,8},{7,9},{8,10},{9,11},{10,... | collective-permute-start | bytes 122888 | tf_op jit(solution)/shard_map/ppermute | solution.py:16
  520.1 8.9 %collective-permute-start.9 = (bf16[20,1024]{1,0:T(8,128)(2,1)S(1)}, bf16[20,1024]{1,0:T(8,128)(2,1)S(1)}, u32[]{:S(2)}, u32[]{:S(2)}) collective-permute-start(bf16[20,1024]{1,0:T(8,128)(2,1)S(1)} %get-tuple-element.30), channel_id=1, source_target_pairs={{0,1},{1,2},{2,3},{3,4},{4,5},{5,6},{6,7},{7,8},{8,9},{9,10},{10,1... | collective-permute-start | bytes 122888 | tf_op jit(solution)/shard_map/ppermute | solution.py:16
Sparse Core Ops, SparseCore 0:
  28.7 67.6 reduce-scatter.9
  346.6 50.4 reduce-scatter.5
  467.0 44.3 reduce-scatter.7
where the time goes:
time: 539 us; the launch traced here: 537 us
  waiting for transfers between devices  374 us (69%)
  starting transfers between devices  59.9 us (11%)
  local copies, waits for them, and re-layouts  45.8 us (8%)
  matrix products  20.6 us (4%)
  blocking collectives  16.2 us (3%)
  between operations  14.1 us (3%)
  other arithmetic  6.24 us (1%)
    ppermute x12, waiting for transfers between devices, passed_along(): return lax.ppermute(x, axis, [(i, (i + by) % count) for i in range(count)])  162 us
    unnamed x4, waiting for transfers between devices  67.9 us
    reduce_scatter x1, waiting for transfers between devices, shards(): lax.psum_scatter(partial_value.astype(jnp.bfloat16), 'rep', scatter_dimen...  50.5 us
    all_to_all x1, waiting for transfers between devices, shards(): lax.all_to_all(outgoing, 'shard', split_axis=0, concat_axis=0, tiled=True)  49.4 us
    ppermute x12, starting transfers between devices, passed_along(): return lax.ppermute(x, axis, [(i, (i + by) % count) for i in range(count)])  46.9 us
    reduce_scatter x1, waiting for transfers between devices, shards(): lax.psum_scatter(partial_two.astype(jnp.bfloat16), 'rep', scatter_dimensi...  44.5 us
    unnamed x19, local copies, waits for them, and re-layouts  26.5 us
    dot_general x2, matrix products, expert_partial(): jnp.einsum('rnd,ngdf->rgf', pieces, weights_in, preferred_element_type=jn...  16.8 us
  transfers between devices with their start and end apart: 16, of which 12 were waited for; matrix products, arithmetic and copies ran while one was open for 0% of the time, Pallas kernels for 0%

commit v1 on v0

v1 whole, which is shorter than its diff:
```python
import jax
import jax.numpy as jnp
from jax import lax
from jax.experimental import pallas as pl
from jax.experimental.pallas import tpu as pltpu
from jax.sharding import PartitionSpec as P

beta_one = 0.9
beta_two = 0.95
learn_rate = 0.05
adam_eps = 1e-08
bias_one = 1.0 - 0.9**10
bias_two = 1.0 - 0.95**10

MESH = pl.DeviceIdType.MESH
F32 = jnp.float32
BF16 = jnp.bfloat16

EXPERTS = 4
D = 4096
SLICE = 32
HID = 384
OWN = 20
PAD = 24
WIDE = 32
GROUP = 8
ROWS = OWN * GROUP
PADDED = PAD * GROUP
CHIP = 2 * PAD
LOCAL = 512
BATCHES = 6
SEG = 128


def div_by(value, count):
    scale = {20: 3277, 24: 2731}[count]
    return (value * scale) >> 16


def iota(shape, dim):
    return lax.broadcasted_iota(jnp.int32, shape, dim)


def one_hot(mask):
    return jnp.where(mask, 1.0, 0.0).astype(BF16)


def dot(a, b):
    return jnp.dot(a, b, preferred_element_type=F32)


def dot_last(a, b):
    return lax.dot_general(a, b, (((1,), (1,)), ((), ())), preferred_element_type=F32)


def wait_bytes(ref, sem):
    pltpu.make_async_copy(ref, ref, sem).wait()


def kernel(
    grads,
    master,
    mom1,
    mom2,
    rows,
    gain,
    ids,
    weights,
    new1,
    new2,
    out,
    W,
    RA,
    SB,
    RR,
    R32,
    XS,
    XR,
    RT,
    PA,
    PB,
    CR,
    TB,
    ZR,
    SQS,
    SQR,
    HB,
    HO,
    YB,
    YR,
    BR,
    OB,
    OR,
    sa_s,
    sa_r,
    sr_s,
    sr_r,
    ag_s,
    ag_r,
    sx_s,
    sx_r,
    st_s,
    st_r,
):
    h = lax.axis_index("rep")
    shard = lax.axis_index("shard")
    c = lax.rem(shard, 2)
    x = lax.rem(lax.div(shard, 2), 4)
    z = lax.rem(lax.div(shard, 8), 4)
    y = lax.div(shard, 32)
    t = z * 2 + c

    def at(yy, zz, xx, cc):
        return ((yy * 4 + zz) * 4 + xx) * 2 + cc

    def ahead(value, by):
        return lax.rem(value + by, 4)

    rep_peers = [(ahead(h, by), shard) for by in (1, 2, 3)]
    x_peers = [(h, at(y, z, ahead(x, by), c)) for by in (1, 2, 3)]
    y_peers = [(h, at(ahead(y, by), z, x, c)) for by in (1, 2, 3)]
    z_steps = [ahead(z, by) for by in (1, 2, 3)]
    z_peers = [(h, at(y, zz, x, c)) for zz in z_steps]
    core_peer = (h, at(y, z, x, 1 - c))
    group_steps = [(zz, c) for zz in z_steps]
    group_steps += [(zz, 1 - c) for zz in [z] + z_steps]
    group_peers = [(h, at(y, zz, x, cc)) for zz, cc in group_steps]

    def send(src, dst, s_sem, r_sem, to):
        pltpu.make_async_remote_copy(
            src_ref=src,
            dst_ref=dst,
            send_sem=s_sem,
            recv_sem=r_sem,
            device_id=to,
            device_id_type=MESH,
        ).start()

    barrier = pltpu.get_barrier_semaphore()
    everyone = rep_peers + x_peers + y_peers + group_peers
    for peer in everyone:
        pl.semaphore_signal(barrier, inc=1, device_id=peer, device_id_type=MESH)

    R32[...] = jnp.zeros(R32.shape, BF16)
    R32[0:OWN, :] = rows[...]
    q = iota((256, 256), 1)
    r = iota((256, 256), 0)
    q_src = ((q & 127) >> 5) * 64 + (q >> 7) * 32 + (q & 31)
    r_src = ((r & 127) >> 5) * 64 + (r >> 7) * 32 + (r & 31)
    perm = one_hot(r == q_src)
    perm_back = one_hot(q == r_src)
    for zz in range(4):
        for yy in range(4):
            first = yy * 1024 + zz * 256
            moved = dot(R32[:, first : first + 256], perm).astype(BF16)
            XS[2 * zz, :, yy * SEG : (yy + 1) * SEG] = moved[:, 0:SEG]
            XS[2 * zz + 1, :, yy * SEG : (yy + 1) * SEG] = moved[:, SEG : 2 * SEG]
    XR[t] = XS[t]
    lane = iota((OWN, 128), 1)
    tile = jnp.zeros((OWN, 128), F32)
    for s in range(2):
        for k in range(2):
            tile = jnp.where(lane == 4 * s + 2 * k, ids[s, :, k : k + 1].astype(F32), tile)
            tile = jnp.where(lane == 4 * s + 2 * k + 1, weights[s, :, k : k + 1], tile)
    RT[t] = jnp.zeros((PAD, 128), F32)
    RT[t, 0:OWN, :] = tile

    def pick(n_to, n_from, to_len, from_len):
        a, b = iota((n_to, n_from), 0), iota((n_to, n_from), 1)
        ta = a >> 5 if to_len == 32 else div_by(a, to_len)
        tb = b >> 5 if from_len == 32 else div_by(b, from_len)
        ia, ib = a - ta * to_len, b - tb * from_len
        return one_hot((ta == tb) & (ia == ib) & (ia < OWN))

    gains = []
    for s in range(2):
        parts = []
        for yy in range(4):
            first = pl.multiple_of(yy * 1024 + z * 256, 256)
            both = dot(gain[:, pl.ds(first, 256)], perm)
            parts.append(jnp.where(c == 0, both[s : s + 1, 0:SEG], both[s : s + 1, SEG : 2 * SEG]))
        gains.append(jnp.concatenate(parts, axis=1))

    pl.semaphore_wait(barrier, len(everyone))

    hp, hm, h2 = ahead(h, 1), ahead(h, 3), ahead(h, 2)
    up_peer, down_peer = (hp, shard), (hm, shard)

    def columns(owner):
        return pl.ds(pl.multiple_of(owner * HID, HID), HID)

    def pieces(b):
        if b < 4:
            return (b, slice(0, 2))
        return (slice(2 * (b - 4), 2 * (b - 4) + 2), 2)

    def grad_at(b, first, last, owner):
        return (0, *pieces(b), slice(first, last), columns(owner))

    def send_across(b):
        send(grads.at[grad_at(b, 0, 16, h2)], RA.at[b, 0], sa_s.at[b, 0], sa_r.at[b, 0], up_peer)
        send(grads.at[grad_at(b, 16, 32, h2)], RA.at[b, 1], sa_s.at[b, 1], sa_r.at[b, 1], down_peer)

    def send_plain(b):
        send(grads.at[grad_at(b, 16, 32, hp)], RR.at[b, 0, :, 16:32], sr_s.at[b, 0], sr_r.at[b, 0], up_peer)
        send(grads.at[grad_at(b, 0, 16, hm)], RR.at[b, 1, :, 0:16], sr_s.at[b, 1], sr_r.at[b, 1], down_peer)

    def send_summed(b):
        wait_bytes(RA.at[b, 0], sa_r.at[b, 0])
        SB[b, 0] = (RA[b, 0].astype(F32) + grads[grad_at(b, 0, 16, hp)].astype(F32)).astype(BF16)
        send(SB.at[b, 0], RR.at[b, 0, :, 0:16], sr_s.at[b, 0], sr_r.at[b, 0], up_peer)
        wait_bytes(RA.at[b, 1], sa_r.at[b, 1])
        SB[b, 1] = (RA[b, 1].astype(F32) + grads[grad_at(b, 16, 32, hm)].astype(F32)).astype(BF16)
        send(SB.at[b, 1], RR.at[b, 1, :, 16:32], sr_s.at[b, 1], sr_r.at[b, 1], down_peer)

    def refit(b):
        wait_bytes(RR.at[b, 0], sr_r.at[b, 0])
        wait_bytes(RR.at[b, 1], sr_r.at[b, 1])
        total = grads[grad_at(b, 0, 32, h)].astype(F32) + RR[b, 0].astype(F32) + RR[b, 1].astype(F32)
        mean = total * 0.25
        where = pieces(b)
        one = beta_one * mom1[where] + (1.0 - beta_one) * mean
        two = beta_two * mom2[where] + (1.0 - beta_two) * mean * mean
        new1[where] = one
        new2[where] = two
        update = one / bias_one / (jnp.sqrt(two / bias_two) + adam_eps)
        W[b, :, y, x] = (master[where] - learn_rate * update).astype(BF16)
        for peer in x_peers:
            send(W.at[b, 0, y, x], W.at[b, 0, y, x], ag_s.at[b, 0, 0], ag_r.at[b, 0, 0], peer)
        for peer in y_peers:
            send(W.at[b, 1, y, x], W.at[b, 1, y, x], ag_s.at[b, 0, 1], ag_r.at[b, 0, 1], peer)

    def pass_on(b):
        wait_bytes(W.at[b, 0, 0, 0:3], ag_r.at[b, 0, 0])
        for peer in y_peers:
            send(W.at[b, 0, y], W.at[b, 0, y], ag_s.at[b, 1, 0], ag_r.at[b, 1, 0], peer)
        wait_bytes(W.at[b, 1, 0, 0:3], ag_r.at[b, 0, 1])
        for peer in x_peers:
            send(W.at[b, 1, :, x], W.at[b, 1, :, x], ag_s.at[b, 1, 1], ag_r.at[b, 1, 1], peer)

    def gathered(b):
        wait_bytes(W.at[b, 0, 0:3], ag_r.at[b, 1, 0])
        wait_bytes(W.at[b, 1, 0:3], ag_r.at[b, 1, 1])

    def rows_in():
        wait_bytes(XR.at[0:7], sx_r.at[0, 0])
        wait_bytes(RT.at[0:7], st_r.at[0])

    def route_column(s, k):
        return RT[...].reshape(PADDED, 128)[:, 4 * s + 2 * k : 4 * s + 2 * k + 1]

    def send_squares(s, raw):
        squares = jnp.sum(raw * raw, axis=1, keepdims=True)
        same = iota((CHIP, 128), 0) == iota((CHIP, 128), 1)
        for zz in range(4):
            part = squares[zz * CHIP : (zz + 1) * CHIP]
            line = jnp.sum(jnp.where(same, part, 0.0), axis=0, keepdims=True)
            SQS[s, zz] = jnp.broadcast_to(line, (8, 128))
        SQR[s, t] = SQS[s, z]
        for (zz, _), peer in zip(group_steps, group_peers):
            send(SQS.at[s, zz], SQR.at[s, t], st_s.at[1 + s], st_r.at[1 + s], peer)

    def first_product(s, e, activations, choice):
        gate = dot(activations, W[e, 0].reshape(LOCAL, HID))
        up = dot(activations, W[e, 1].reshape(LOCAL, HID))
        for k in range(2):
            chosen = choice[k] == float(e)
            PA[k, 0] = PA[k, 0] + jnp.where(chosen, gate, 0.0)
            PA[k, 1] = PA[k, 1] + jnp.where(chosen, up, 0.0)

    def swap_cores(s):
        PB[s] = PA[...].astype(BF16)
        send(PB.at[s, 1 - c], CR.at[s], sx_s.at[1, s], sx_r.at[1, s], core_peer)

    def sum_group(s):
        wait_bytes(CR.at[s], sx_r.at[1, s])
        for g in range(2):
            both = PB[s, c, g].astype(F32) + CR[s, g].astype(F32)
            for zz in range(4):
                TB[s, zz, g] = both[zz * CHIP : (zz + 1) * CHIP].astype(BF16)
        for zz, peer in zip(z_steps, z_peers):
            send(TB.at[s, zz], ZR.at[s, z], sx_s.at[2, s], sx_r.at[2, s], peer)
        ZR[s, z] = TB[s, z]

    def hidden_units(s):
        wait_bytes(SQR.at[s, 0:7], st_r.at[1 + s])
        total = jnp.sum(SQR[s][:, 0, :], axis=0, keepdims=True)
        scale_line = lax.rsqrt(total / float(D) + 1e-06)
        same = iota((CHIP, 128), 0) == iota((CHIP, 128), 1)
        scale = jnp.sum(jnp.where(same, scale_line, 0.0), axis=1, keepdims=True)
        routes = RT[pl.ds(2 * z, 2)].reshape(CHIP, 128)
        share = jnp.where(c == 0, routes[:, 4 * s + 1 : 4 * s + 2], routes[:, 4 * s + 3 : 4 * s + 4])
        wait_bytes(ZR.at[s, 0:3], sx_r.at[2, s])
        parts = [ZR[s, zz].astype(F32) for zz in range(4)]
        both = (parts[0] + parts[1]) + (parts[2] + parts[3])
        gate, up = both[0] * scale, both[1] * scale
        HB[s, z] = (jax.nn.silu(gate) * up * share).astype(BF16)
        for peer in z_peers:
            send(HB.at[s, z], HB.at[s, z], sx_s.at[3, s], sx_r.at[3, s], peer)

    def swap_hidden(s):
        wait_bytes(HB.at[s, 0:3], sx_r.at[3, s])
        send(HB.at[s], HO.at[s], sx_s.at[4, s], sx_r.at[4, s], core_peer)

    def second_product(packed, choice, total):
        for e in range(EXPERTS):
            mine = jnp.where(choice == float(e), packed, 0.0).astype(BF16)
            part = dot_last(mine, W[4 + e // 2, e % 2].reshape(LOCAL, HID))
            total = part if total is None else total + part
        return total

    def send_sums(s, total):
        for hh in range(4):
            YB[s, hh] = total[:, hh * SEG : (hh + 1) * SEG].astype(BF16)
        for peer in rep_peers:
            send(YB.at[s, peer[0]], YR.at[s, h], sx_s.at[5, s], sx_r.at[5, s], peer)
        YR[s, h] = YB[s, h]

    def branch_part(s):
        wait_bytes(YR.at[s, 0:3], sx_r.at[5, s])
        parts = [YR[s, hh].astype(F32) for hh in range(4)]
        return ((parts[0] + parts[1]) + (parts[2] + parts[3])).astype(BF16)

    def send_home(s, part, spread):
        OB[s] = dot(spread, part).astype(BF16).reshape(GROUP, WIDE, SEG)
        OR[s, t] = OB[s, t]
        for (zz, cc), peer in zip(group_steps, group_peers):
            send(OB.at[s, 2 * zz + cc], OR.at[s, t], sx_s.at[6, s], sx_r.at[6, s], peer)

    def store_home(s):
        wait_bytes(OR.at[s, 0:7], sx_r.at[6, s])
        for zz in range(4):
            both = jnp.concatenate([OR[s, 2 * zz], OR[s, 2 * zz + 1]], axis=1)
            out[s, :, zz * 256 : (zz + 1) * 256] = dot(both, perm_back).astype(BF16)[0:OWN]

    send_across(0)
    send_plain(0)
    send_across(1)
    for (zz, cc), peer in zip(group_steps, group_peers):
        send(XS.at[2 * zz + cc], XR.at[t], sx_s.at[0, 0], sx_r.at[0, 0], peer)
        send(RT.at[t], RT.at[t], st_s.at[0], st_r.at[0], peer)

    def first_rows():
        rows_in()
        arrived = XR[...].reshape(GROUP * WIDE, LOCAL)
        raw_packed = dot(pick(ROWS, GROUP * WIDE, OWN, WIDE), arrived)
        raw = dot(pick(PADDED, GROUP * WIDE, PAD, WIDE), arrived)
        return raw_packed, raw

    for b in range(BATCHES + 1):
        if b < BATCHES:
            send_summed(b)
            if b + 1 < BATCHES:
                send_plain(b + 1)
            if b + 2 < BATCHES:
                send_across(b + 2)
        if b >= 1:
            refit(b - 1)
        if b >= 2:
            pass_on(b - 2)
        if b == 2:
            raw_packed, raw = first_rows()
            send_squares(0, raw)
            acts = (raw * gains[0]).astype(BF16)
            choice = [route_column(0, k) for k in range(2)]
            PA[...] = jnp.zeros(PA.shape, F32)
        if 3 <= b < 3 + EXPERTS:
            gathered(b - 3)
            first_product(0, b - 3, acts, choice)

    pack = pick(ROWS, PADDED, OWN, PAD)
    unpack = pick(PADDED, ROWS, PAD, OWN)
    spread = pick(GROUP * WIDE, ROWS, WIDE, OWN)
    routes_packed = dot(pack, RT[...].reshape(PADDED, 128).astype(BF16))

    def packed_choice(s, k):
        return routes_packed[:, 4 * s + 2 * k : 4 * s + 2 * k + 1]

    def rest_of_step(s):
        own_choice = jnp.where(c == 0, packed_choice(s, 0), packed_choice(s, 1))
        other_choice = jnp.where(c == 0, packed_choice(s, 1), packed_choice(s, 0))
        swap_hidden(s)
        total = second_product(dot(pack, HB[s].reshape(PADDED, HID)), own_choice, None)
        wait_bytes(HO.at[s], sx_r.at[4, s])
        total = second_product(dot(pack, HO[s].reshape(PADDED, HID)), other_choice, total)
        send_sums(s, total)
        return branch_part(s)

    swap_cores(0)
    pass_on(BATCHES - 1)
    sum_group(0)
    hidden_units(0)
    gathered(4)
    gathered(5)
    part = rest_of_step(0)

    BR[h] = part
    for peer in rep_peers:
        send(BR.at[h], BR.at[h], sx_s.at[0, 1], sx_r.at[0, 1], peer)
    send_home(0, part, spread)
    wait_bytes(BR.at[0:3], sx_r.at[0, 1])
    branch = jnp.concatenate([BR[hh] for hh in range(4)], axis=1).astype(F32)
    middle = (raw_packed + branch).astype(BF16)
    raw = dot(unpack, middle)
    send_squares(1, raw)
    acts = (raw * gains[1]).astype(BF16)
    choice = [route_column(1, k) for k in range(2)]
    PA[...] = jnp.zeros(PA.shape, F32)
    for e in range(EXPERTS):
        first_product(1, e, acts, choice)
    swap_cores(1)
    sum_group(1)
    hidden_units(1)
    part = rest_of_step(1)
    send_home(1, part, spread)
    store_home(0)
    store_home(1)

    for b in range(BATCHES):
        for way in range(2):
            wait_bytes(RA.at[b, way], sa_s.at[b, way])
            wait_bytes(RR.at[b, way], sr_s.at[b, way])
        for p in range(2):
            wait_bytes(W.at[b, p, 0, 0:3], ag_s.at[b, 0, p])
            wait_bytes(W.at[b, p, 0:3], ag_s.at[b, 1, p])
    wait_bytes(XS.at[0:7], sx_s.at[0, 0])
    wait_bytes(RT.at[0:7], st_s.at[0])
    wait_bytes(BR.at[0:3], sx_s.at[0, 1])
    for s in range(2):
        wait_bytes(SQR.at[s, 0:7], st_s.at[1 + s])
        wait_bytes(CR.at[s], sx_s.at[1, s])
        wait_bytes(ZR.at[s, 0:3], sx_s.at[2, s])
        wait_bytes(HB.at[s, 0:3], sx_s.at[3, s])
        wait_bytes(HO.at[s], sx_s.at[4, s])
        wait_bytes(YR.at[s, 0:3], sx_s.at[5, s])
        wait_bytes(OR.at[s, 0:7], sx_s.at[6, s])


def shards(grad_stack, master_weight, moment_one, moment_two, decode_rows, norm_gain, route_ids, route_weights):
    dma = pltpu.SemaphoreType.DMA
    vmem = pltpu.VMEM
    scratch = [
        vmem((BATCHES, 2, 4, 4, SLICE, HID), BF16),
        vmem((BATCHES, 2, 2, 16, HID), BF16),
        vmem((BATCHES, 2, 2, 16, HID), BF16),
        vmem((BATCHES, 2, 2, SLICE, HID), BF16),
        vmem((WIDE, D), BF16),
        vmem((GROUP, WIDE, LOCAL), BF16),
        vmem((GROUP, WIDE, LOCAL), BF16),
        vmem((GROUP, PAD, 128), F32),
        vmem((2, 2, PADDED, HID), F32),
        vmem((2, 2, 2, PADDED, HID), BF16),
        vmem((2, 2, PADDED, HID), BF16),
        vmem((2, 4, 2, CHIP, HID), BF16),
        vmem((2, 4, 2, CHIP, HID), BF16),
        vmem((2, 4, 8, 128), F32),
        vmem((2, GROUP, 8, 128), F32),
        vmem((2, 4, CHIP, HID), BF16),
        vmem((2, 4, CHIP, HID), BF16),
        vmem((2, 4, ROWS, SEG), BF16),
        vmem((2, 4, ROWS, SEG), BF16),
        vmem((4, ROWS, SEG), BF16),
        vmem((2, GROUP, WIDE, SEG), BF16),
        vmem((2, GROUP, WIDE, SEG), BF16),
        dma((BATCHES, 2)),
        dma((BATCHES, 2)),
        dma((BATCHES, 2)),
        dma((BATCHES, 2)),
        dma((BATCHES, 2, 2)),
        dma((BATCHES, 2, 2)),
        dma((7, 2)),
        dma((7, 2)),
        dma((3,)),
        dma((3,)),
    ]
    in_vmem = pl.BlockSpec(memory_space=pltpu.VMEM)
    return pl.pallas_call(
        kernel,
        out_shape=(
            jax.ShapeDtypeStruct(moment_one.shape, F32),
            jax.ShapeDtypeStruct(moment_two.shape, F32),
            jax.ShapeDtypeStruct((2, OWN, D // 4), BF16),
        ),
        in_specs=[in_vmem] * 8,
        out_specs=(in_vmem,) * 3,
        scratch_shapes=scratch,
        compiler_params=pltpu.CompilerParams(
            collective_id=0, has_side_effects=True, vmem_limit_bytes=40 * 1024 * 1024
        ),
        name="refit_and_decode",
    )(grad_stack, master_weight, moment_one, moment_two, decode_rows, norm_gain, route_ids, route_weights)


def solution(mesh):
    return jax.shard_map(
        shards,
        mesh=mesh,
        in_specs=(
            P("rep", None, None, "shard", None),
            P(None, None, "shard", "rep"),
            P(None, None, "shard", "rep"),
            P(None, None, "shard", "rep"),
            P("shard", None),
            P(),
            P(None, "shard", None),
            P(None, "shard", None),
        ),
        out_specs=(
            P(None, None, "shard", "rep"),
            P(None, None, "shard", "rep"),
            P(None, "shard", "rep"),
        ),
        check_vma=False,
    )
```

time: 539 us -> 158 us (0.29)
  waiting for transfers between devices: 374 us -> 0 us
  Pallas kernels: 0 us -> 147 us
  starting transfers between devices: 59.9 us -> 0 us
  local copies, waits for them, and re-layouts: 45.8 us -> 10 us
  matrix products: 20.6 us -> 0 us
  blocking collectives: 16.2 us -> 0 us
  between operations: 14.1 us -> 0.65 us
  other arithmetic: 6.24 us -> 0 us
    ppermute x12 -> x0, waiting for transfers between devices: 162 us -> none  [passed_along(): return lax.ppermute(x, axis, [(i, (i + by) % count) for i in range(count)])]
    pallas_call x0 -> x1, Pallas kernels: none -> 147 us  [shards(): pl.pallas_call(kernel, out_shape=(jax.ShapeDtypeStruct(moment_one.shape,...]
    reduce_scatter x2 -> x0, waiting for transfers between devices: 95 us -> none  [the longest x1 50.5 us: shards(): lax.psum_scatter(partial_value.astype(jnp.bfloat16), 'rep', scatter_dimen...]
    unnamed x4 -> x0, waiting for transfers between devices: 67.9 us -> none
    all_to_all x1 -> x0, waiting for transfers between devices: 49.4 us -> none  [shards(): lax.all_to_all(outgoing, 'shard', split_axis=0, concat_axis=0, tiled=True)]
    ppermute x12 -> x0, starting transfers between devices: 46.9 us -> none  [passed_along(): return lax.ppermute(x, axis, [(i, (i + by) % count) for i in range(count)])]
    dot_general x4 -> x0, matrix products: 20.6 us -> none  [the longest x2 16.8 us: expert_partial(): jnp.einsum('rnd,ngdf->rgf', pieces, weights_in, preferred_element_type=jn...]
    unnamed x19 -> x16, local copies, waits for them, and re-layouts: 26.5 us -> 9.29 us
  transfers between devices with their start and end apart: 16 -> 0, of which waited for: 12 -> 0; matrix products, arithmetic and copies ran while one was open for 0% -> 0% of each run, Pallas kernels for 0% -> 0%
where the time goes in v1:
time: 158 us; the launch traced here: 157 us
  Pallas kernels  147 us (93%)
  local copies, waits for them, and re-layouts  10 us (6%)
    pallas_call x1, Pallas kernels, shards(): pl.pallas_call(kernel, out_shape=(jax.ShapeDtypeStruct(moment_one.shape,...  147 us
    unnamed x16, local copies, waits for them, and re-layouts  9.29 us

profile of v1, /device:TPU:1, one launch (start us, length us, event | category | flops | bytes accessed | tf_op | source)
XLA Modules:
  0.0 157.4 jit_solution(6211024592536365225)
XLA Ops:
  0.6 0.8 copy.11.ids
  1.4 0.8 copy.12.weights
  2.2 0.0 copy-start
  2.2 1.3 copy-done
  3.5 0.0 copy-start.1
  3.5 1.1 copy-done.1
  4.5 0.0 copy-start.2
  4.5 1.1 copy-done.2
  5.6 0.0 copy-start.3
  5.6 1.1 copy-done.3
  6.7 0.0 copy-start.4
  6.7 0.9 copy-done.4
  7.6 0.0 copy-start.5
  7.6 0.7 copy-done.5
  8.3 146.8 %refit_and_decode.1 = (f32[4,3,32,384]{3,2,1,0:T(8,128)S(1)}, f32[4,3,32,384]{3,2,1,0:T(8,128)S(1)}, bf16[2,20,1024]{2,1,0:T(8,128)(2,1)S(1)}) custom-call(bf16[1,4,3,32,1536]{4,3,2,1,0:T(8,128)(2,1)S(1)} %copy-done, f32[4,3,32,384]{3,2,1,0:T(8,128)S(1)} %copy-done.1, f32[4,3,32,384]{3,2,1,0:T(8,128)S(1)} %copy-done.2, f32[4,3,32,384]{3,2,1,0:T(8,128)S(1)} %copy-done.3, ...), custom_call_target="tpu_custom_call" | custom-call | tf_op jit(solution)/shard_map/refit_and_decode/pallas_call | solution.py:477
  155.1 0.7 copy.13
  155.8 0.8 copy.16
  156.6 0.8 copy.17
Async XLA Ops:
  2.2 1.3 copy-start
  3.5 1.1 copy-start.1
  4.5 1.1 copy-start.2
  5.6 1.1 copy-start.3
  6.7 0.9 copy-start.4
  7.6 0.7 copy-start.5

commit v2 on v1

v2 whole, which is shorter than its diff:
```python
import jax
import jax.numpy as jnp
from jax import lax
from jax.experimental import pallas as pl
from jax.experimental.pallas import tpu as pltpu
from jax.sharding import PartitionSpec as P

beta_one = 0.9
beta_two = 0.95
learn_rate = 0.05
adam_eps = 1e-08
bias_one = 1.0 - 0.9**10
bias_two = 1.0 - 0.95**10

MESH = pl.DeviceIdType.MESH
F32 = jnp.float32
BF16 = jnp.bfloat16

EXPERTS = 4
D = 4096
SLICE = 32
HID = 384
OWN = 20
PAD = 24
WIDE = 32
GROUP = 8
ROWS = OWN * GROUP
PADDED = PAD * GROUP
HALF = PADDED // 2
HALF_ROWS = ROWS // 2
BOTH = 2 * PAD
PACKED = 80
LOCAL = 512
BATCHES = 6
SEG = 128


def div_by(value, count):
    scale = {20: 3277, 24: 2731}[count]
    return (value * scale) >> 16


def iota(shape, dim):
    return lax.broadcasted_iota(jnp.int32, shape, dim)


def one_hot(mask):
    return jnp.where(mask, 1.0, 0.0).astype(BF16)


def dot(a, b):
    return jnp.dot(a, b, preferred_element_type=F32)


def dot_last(a, b):
    return lax.dot_general(a, b, (((1,), (1,)), ((), ())), preferred_element_type=F32)


def wait_bytes(ref, sem):
    pltpu.make_async_copy(ref, ref, sem).wait()


def kernel(
    grads,
    master,
    mom1,
    mom2,
    rows,
    gain,
    ids,
    weights,
    new1,
    new2,
    out,
    GV,
    MV,
    N1,
    N2,
    W,
    RA,
    SB,
    RR,
    RV,
    GN,
    IV,
    WV,
    R32,
    XS,
    XR,
    RT,
    PA,
    PB,
    CR,
    TB,
    ZR,
    SQS,
    SQR,
    HB,
    HO,
    YB,
    YR,
    BR,
    OB,
    OR,
    in_sem,
    out_sem,
    sa_s,
    sa_r,
    sr_s,
    sr_r,
    ag_s,
    ag_r,
    sx_s,
    sx_r,
    st_s,
    st_r,
):
    h = lax.axis_index("rep")
    shard = lax.axis_index("shard")
    c = lax.rem(shard, 2)
    x = lax.rem(lax.div(shard, 2), 4)
    z = lax.rem(lax.div(shard, 8), 4)
    y = lax.div(shard, 32)
    t = c * 4 + z

    def at(yy, zz, xx, cc):
        return ((yy * 4 + zz) * 4 + xx) * 2 + cc

    def ahead(value, by):
        return lax.rem(value + by, 4)

    rep_peers = [(ahead(h, by), shard) for by in (1, 2, 3)]
    x_peers = [(h, at(y, z, ahead(x, by), c)) for by in (1, 2, 3)]
    y_peers = [(h, at(ahead(y, by), z, x, c)) for by in (1, 2, 3)]
    z_steps = [ahead(z, by) for by in (1, 2, 3)]
    z_peers = [(h, at(y, zz, x, c)) for zz in z_steps]
    core_peer = (h, at(y, z, x, 1 - c))
    group_steps = [(zz, c) for zz in z_steps]
    group_steps += [(zz, 1 - c) for zz in [z] + z_steps]
    group_peers = [(h, at(y, zz, x, cc)) for zz, cc in group_steps]

    place = 4 * h + z

    def near(by, cc):
        there = lax.rem(place + by + 16, 16)
        return (lax.div(there, 4), at(y, lax.rem(there, 4), x, cc))

    two = jnp.where(lax.rem(place, 2) == 0, 2, -2)
    near_steps = [(by, cc) for by in (1, -1, two) for cc in (0, 1)]

    def send(src, dst, s_sem, r_sem, to):
        pltpu.make_async_remote_copy(
            src_ref=src,
            dst_ref=dst,
            send_sem=s_sem,
            recv_sem=r_sem,
            device_id=to,
            device_id_type=MESH,
        ).start()

    barrier = pltpu.get_barrier_semaphore()
    everyone = rep_peers + x_peers + y_peers + group_peers
    everyone += [near(by, cc) for by in (1, -1, 2, -2) for cc in (0, 1)]
    for peer in everyone:
        pl.semaphore_signal(barrier, inc=1, device_id=peer, device_id_type=MESH)
    incoming = [
        pltpu.make_async_copy(grads.at[0], GV, in_sem.at[0]),
        pltpu.make_async_copy(rows, RV, in_sem.at[1]),
        pltpu.make_async_copy(gain, GN, in_sem.at[2]),
        pltpu.make_async_copy(ids, IV, in_sem.at[3]),
        pltpu.make_async_copy(master, MV.at[0], in_sem.at[4]),
        pltpu.make_async_copy(mom1, MV.at[1], in_sem.at[5]),
        pltpu.make_async_copy(mom2, MV.at[2], in_sem.at[6]),
        pltpu.make_async_copy(weights, WV, in_sem.at[7]),
    ]
    for copy in incoming:
        copy.start()

    def pick(n_to, n_from, to_len, from_len):
        a, b = iota((n_to, n_from), 0), iota((n_to, n_from), 1)
        ta = a >> 5 if to_len == 32 else div_by(a, to_len)
        tb = b >> 5 if from_len == 32 else div_by(b, from_len)
        ia, ib = a - ta * to_len, b - tb * from_len
        return one_hot((ta == tb) & (ia == ib) & (ia < OWN))

    hp, hm, h2 = ahead(h, 1), ahead(h, 3), ahead(h, 2)
    up_peer, down_peer = (hp, shard), (hm, shard)

    def columns(owner):
        return pl.ds(pl.multiple_of(owner * HID, HID), HID)

    def pieces(b):
        if b < 4:
            return (b, slice(0, 2))
        return (slice(2 * (b - 4), 2 * (b - 4) + 2), 2)

    def grad_at(b, first, last, owner):
        return (*pieces(b), slice(first, last), columns(owner))

    def send_across(b):
        send(GV.at[grad_at(b, 0, 16, h2)], RA.at[b, 0], sa_s.at[b, 0], sa_r.at[b, 0], up_peer)
        send(GV.at[grad_at(b, 16, 32, h2)], RA.at[b, 1], sa_s.at[b, 1], sa_r.at[b, 1], down_peer)

    def send_plain(b):
        src = GV.at[grad_at(b, 16, 32, hp)]
        send(src, RR.at[b, 0, :, 16:32], sr_s.at[b, 0], sr_r.at[b, 0], up_peer)
        src = GV.at[grad_at(b, 0, 16, hm)]
        send(src, RR.at[b, 1, :, 0:16], sr_s.at[b, 1], sr_r.at[b, 1], down_peer)

    def send_summed(b):
        wait_bytes(RA.at[b, 0], sa_r.at[b, 0])
        SB[b, 0] = (RA[b, 0].astype(F32) + GV[grad_at(b, 0, 16, hp)].astype(F32)).astype(BF16)
        send(SB.at[b, 0], RR.at[b, 0, :, 0:16], sr_s.at[b, 0], sr_r.at[b, 0], up_peer)
        wait_bytes(RA.at[b, 1], sa_r.at[b, 1])
        SB[b, 1] = (RA[b, 1].astype(F32) + GV[grad_at(b, 16, 32, hm)].astype(F32)).astype(BF16)
        send(SB.at[b, 1], RR.at[b, 1, :, 16:32], sr_s.at[b, 1], sr_r.at[b, 1], down_peer)

    def refit(b):
        wait_bytes(RR.at[b, 0], sr_r.at[b, 0])
        wait_bytes(RR.at[b, 1], sr_r.at[b, 1])
        total = GV[grad_at(b, 0, 32, h)].astype(F32) + RR[b, 0].astype(F32) + RR[b, 1].astype(F32)
        mean = total * 0.25
        where = pieces(b)
        one = beta_one * MV[(1, *where)] + (1.0 - beta_one) * mean
        two = beta_two * MV[(2, *where)] + (1.0 - beta_two) * mean * mean
        update = one / bias_one / (jnp.sqrt(two / bias_two) + adam_eps)
        W[b, :, y, x] = (MV[(0, *where)] - learn_rate * update).astype(BF16)
        for peer in x_peers:
            send(W.at[b, 0, y, x], W.at[b, 0, y, x], ag_s.at[b, 0, 0], ag_r.at[b, 0, 0], peer)
        for peer in y_peers:
            send(W.at[b, 1, y, x], W.at[b, 1, y, x], ag_s.at[b, 0, 1], ag_r.at[b, 0, 1], peer)
        N1[where] = one
        N2[where] = two
        pltpu.make_async_copy(N1.at[where], new1.at[where], out_sem.at[b, 0]).start()
        pltpu.make_async_copy(N2.at[where], new2.at[where], out_sem.at[b, 1]).start()

    def pass_on(b):
        wait_bytes(W.at[b, 0, 0, 0:3], ag_r.at[b, 0, 0])
        for peer in y_peers:
            send(W.at[b, 0, y], W.at[b, 0, y], ag_s.at[b, 1, 0], ag_r.at[b, 1, 0], peer)
        wait_bytes(W.at[b, 1, 0, 0:3], ag_r.at[b, 0, 1])
        for peer in x_peers:
            send(W.at[b, 1, :, x], W.at[b, 1, :, x], ag_s.at[b, 1, 1], ag_r.at[b, 1, 1], peer)

    def gathered(b):
        wait_bytes(W.at[b, 0, 0:3], ag_r.at[b, 1, 0])
        wait_bytes(W.at[b, 1, 0:3], ag_r.at[b, 1, 1])

    def permutations():
        q = iota((256, 256), 1)
        r = iota((256, 256), 0)
        q_src = ((q & 127) >> 5) * 64 + (q >> 7) * 32 + (q & 31)
        r_src = ((r & 127) >> 5) * 64 + (r >> 7) * 32 + (r & 31)
        return one_hot(r == q_src), one_hot(q == r_src)

    def cut_rows():
        R32[...] = jnp.zeros(R32.shape, BF16)
        perm = permutations()[0]
        incoming[3].wait()
        incoming[7].wait()
        diagonal = iota((PAD, OWN), 0) == iota((PAD, OWN), 1)
        lane = iota((PAD, 128), 1)
        tile = jnp.zeros((PAD, 128), F32)
        for s in range(2):
            for k in range(2):
                for first, line in ((0, IV[s, k : k + 1].astype(F32)), (4, WV[s, k : k + 1])):
                    column = jnp.sum(jnp.where(diagonal, line, 0.0), axis=1, keepdims=True)
                    tile = jnp.where(lane == first + 2 * s + k, column, tile)
        RT[t] = tile
        incoming[1].wait()
        R32[0:OWN, :] = RV[...]
        blocks = [R32[:, (4 * yy + zz) * 256 : (4 * yy + zz + 1) * 256] for zz in range(4) for yy in range(4)]
        moved = dot(jnp.concatenate(blocks, axis=0), perm).astype(BF16)
        moved = dot(pick(16 * OWN, 16 * WIDE, OWN, WIDE), moved).astype(BF16)
        for zz in range(4):
            XS[zz] = moved[4 * zz * OWN : 4 * (zz + 1) * OWN, 0:SEG]
            XS[4 + zz] = moved[4 * zz * OWN : 4 * (zz + 1) * OWN, SEG : 2 * SEG]
        XR[t] = XS[t]

    def send_rows():
        for by, cc in near_steps:
            zz = lax.rem(place + by + 16, 4)
            send(XS.at[4 * cc + zz], XR.at[t], sx_s.at[0, 0], sx_r.at[0, 0], near(by, cc))
            send(RT.at[t], RT.at[t], st_s.at[0], st_r.at[0], near(by, cc))
        send(XS.at[4 * (1 - c) + z], XR.at[t], sx_s.at[0, 0], sx_r.at[0, 0], core_peer)
        send(RT.at[t], RT.at[t], st_s.at[0], st_r.at[0], core_peer)

    def local_gains():
        incoming[2].wait()
        perm = permutations()[0]
        gains = [[], []]
        for yy in range(4):
            first = pl.multiple_of(yy * 1024 + z * 256, 256)
            both = dot(GN[:, pl.ds(first, 256)], perm)
            both = jnp.where(c == 0, both[:, 0:SEG], both[:, SEG : 2 * SEG])
            for s in range(2):
                gains[s].append(both[s : s + 1])
        return [jnp.concatenate(parts, axis=1) for parts in gains]

    def first_rows():
        wait_bytes(XR.at[0:7], sx_r.at[0, 0])
        wait_bytes(RT.at[0:7], st_r.at[0])
        a, b = iota((4 * ROWS, 4 * ROWS), 0), iota((4 * ROWS, 4 * ROWS), 1)
        to_y = sum(jnp.where(a >= n * ROWS, 1, 0) for n in (1, 2, 3))
        to_t = div_by(a - to_y * ROWS, OWN)
        source = to_t * (4 * OWN) + to_y * OWN + (a - to_y * ROWS - to_t * OWN)
        arrived = dot(one_hot(b == source), XR[...].reshape(4 * ROWS, SEG))
        raw_packed = jnp.concatenate([arrived[n * ROWS : (n + 1) * ROWS] for n in range(4)], axis=1)
        raw = dot(pick(PADDED, ROWS, PAD, OWN), raw_packed.astype(BF16))
        return raw_packed, raw

    def route_column(s, k):
        return RT[...].reshape(PADDED, 128)[:, 2 * s + k : 2 * s + k + 1]

    same = iota((PAD, 128), 0) == iota((PAD, 128), 1)

    def send_squares(s, half, raw):
        squares = jnp.sum(raw * raw, axis=1, keepdims=True)
        for zz in range(4):
            part = squares[zz * PAD : (zz + 1) * PAD]
            line = jnp.sum(jnp.where(same, part, 0.0), axis=0, keepdims=True)
            SQS[s, half, zz] = jnp.broadcast_to(line, (8, 128))
        SQR[s, half, t] = SQS[s, half, z]
        for (zz, _), peer in zip(group_steps, group_peers):
            src = SQS.at[s, half, zz]
            send(src, SQR.at[s, half, t], st_s.at[1 + 2 * s + half], st_r.at[1 + 2 * s + half], peer)

    def first_product(e, activations, choice, first, count):
        gate = dot(activations, W[e, 0].reshape(LOCAL, HID))
        up = dot(activations, W[e, 1].reshape(LOCAL, HID))
        for k in range(2):
            chosen = choice[k] == float(e)
            for g, value in enumerate((gate, up)):
                value = jnp.where(chosen, value, 0.0)
                if e > 0:
                    value = PA[k, g, first : first + count] + value
                PA[k, g, first : first + count] = value

    def swap_cores(s, half):
        for k in range(2):
            for g in range(2):
                PB[s, half, k, g] = PA[k, g, half * HALF : (half + 1) * HALF].astype(BF16)
        send(PB.at[s, half, 1 - c], CR.at[s, half], sx_s.at[1 + half, s], sx_r.at[1 + half, s], core_peer)

    def sum_group(s, half):
        wait_bytes(CR.at[s, half], sx_r.at[1 + half, s])
        gate = PB[s, half, c, 0].astype(F32) + CR[s, half, 0].astype(F32)
        up = PB[s, half, c, 1].astype(F32) + CR[s, half, 1].astype(F32)
        for zz in range(4):
            cut = slice(zz * PAD, (zz + 1) * PAD)
            TB[s, half, zz] = jnp.concatenate([gate[cut], up[cut]], axis=0).astype(BF16)
        for zz, peer in zip(z_steps, z_peers):
            send(TB.at[s, half, zz], ZR.at[s, half, z], sx_s.at[3 + half, s], sx_r.at[3 + half, s], peer)
        ZR[s, half, z] = TB[s, half, z]

    def hidden_units(s, half):
        wait_bytes(SQR.at[s, half, 0:7], st_r.at[1 + 2 * s + half])
        total = jnp.sum(SQR[s, half][:, 0, :], axis=0, keepdims=True)
        scale_line = lax.rsqrt(total / float(D) + 1e-06)
        scale = jnp.sum(jnp.where(same, scale_line, 0.0), axis=1, keepdims=True)
        routes = RT[4 * half + z]
        share = jnp.where(c == 0, routes[:, 4 + 2 * s : 5 + 2 * s], routes[:, 5 + 2 * s : 6 + 2 * s])
        wait_bytes(ZR.at[s, half, 0:3], sx_r.at[3 + half, s])
        parts = [ZR[s, half, zz].astype(F32) for zz in range(4)]
        both = (parts[0] + parts[1]) + (parts[2] + parts[3])
        gate, up = both[0:PAD] * scale, both[PAD:BOTH] * scale
        units = jax.nn.silu(gate) * up * share
        blocks = [units[:, i * 128 : (i + 1) * 128] for i in range(3)]
        blocks.append(jnp.zeros((PACKED - 3 * PAD, 128), F32))
        HB[s, half, z] = jnp.concatenate(blocks, axis=0).astype(BF16)
        for peer in z_peers:
            send(HB.at[s, half, z], HB.at[s, half, z], sx_s.at[5 + half, s], sx_r.at[5 + half, s], peer)

    def swap_hidden(s, half):
        wait_bytes(HB.at[s, half, 0:3], sx_r.at[5 + half, s])
        send(HB.at[s, half], HO.at[s, half], sx_s.at[7 + half, s], sx_r.at[7 + half, s], core_peer)

    def second_product(units, choice, total):
        flat = dot(pack, units.reshape(4 * PACKED, 128))
        flat = jnp.concatenate([flat[i * HALF_ROWS : (i + 1) * HALF_ROWS] for i in range(3)], axis=1)
        for e in range(EXPERTS):
            mine = jnp.where(choice == float(e), flat, 0.0).astype(BF16)
            part = dot_last(mine, W[4 + e // 2, e % 2].reshape(LOCAL, HID))
            total = part if total is None else total + part
        return total

    def send_sums(s, half, total):
        for hh in range(4):
            YB[s, half, hh] = total[:, hh * SEG : (hh + 1) * SEG].astype(BF16)
        for peer in rep_peers:
            src = YB.at[s, half, peer[0]]
            send(src, YR.at[s, half, h], sx_s.at[9 + half, s], sx_r.at[9 + half, s], peer)
        YR[s, half, h] = YB[s, half, h]

    def branch_part(s, half):
        wait_bytes(YR.at[s, half, 0:3], sx_r.at[9 + half, s])
        parts = [YR[s, half, hh].astype(F32) for hh in range(4)]
        return ((parts[0] + parts[1]) + (parts[2] + parts[3])).astype(BF16)

    def share_part(half, part):
        BR[half, h] = part
        for peer in rep_peers:
            send(BR.at[half, h], BR.at[half, h], sx_s.at[11, half], sx_r.at[11, half], peer)

    def middle_rows(half):
        wait_bytes(BR.at[half, 0:3], sx_r.at[11, half])
        branch = jnp.concatenate([BR[half, hh] for hh in range(4)], axis=1).astype(F32)
        middle = (raw_packed[half * HALF_ROWS : (half + 1) * HALF_ROWS] + branch).astype(BF16)
        return dot(unpack, middle)

    def send_home(s, half, part):
        OB[s, 4 * half : 4 * half + 4] = dot(spread, part).astype(BF16).reshape(4, WIDE, SEG)

        @pl.when(c == half)
        def _():
            OR[s, t] = OB[s, t]
            for zz, peer in zip(z_steps, z_peers):
                send(OB.at[s, 4 * half + zz], OR.at[s, t], sx_s.at[12, s], sx_r.at[12, s], peer)

        @pl.when(c != half)
        def _():
            for zz in [z] + z_steps:
                peer = (h, at(y, zz, x, half))
                send(OB.at[s, 4 * half + zz], OR.at[s, t], sx_s.at[12, s], sx_r.at[12, s], peer)

    def store_home(s):
        wait_bytes(OR.at[s, 0:7], sx_r.at[12, s])
        perm_back = permutations()[1]
        for zz in range(4):
            both = jnp.concatenate([OR[s, zz], OR[s, 4 + zz]], axis=1)
            out[s, :, zz * 256 : (zz + 1) * 256] = dot(both, perm_back).astype(BF16)[0:OWN]

    cut_rows()
    incoming[0].wait()
    pl.semaphore_wait(barrier, len(everyone))
    send_across(0)
    send_plain(0)
    send_across(1)
    gains = local_gains()
    send_summed(0)
    send_plain(1)
    send_across(2)
    send_summed(1)
    send_plain(2)
    send_across(3)
    for copy in incoming[4:7]:
        copy.wait()
    refit(0)
    send_summed(2)
    send_plain(3)
    pass_on(0)
    refit(1)
    send_summed(3)
    send_across(4)
    send_plain(4)
    send_rows()
    send_across(5)
    send_plain(5)
    pass_on(1)
    refit(2)
    refit(3)
    pass_on(2)
    send_summed(4)
    pass_on(3)
    raw_packed, raw = first_rows()
    acts = (raw * gains[0]).astype(BF16)
    choice = [route_column(0, k) for k in range(2)]
    for half in range(2):
        send_squares(0, half, raw[half * HALF : (half + 1) * HALF])
    send_summed(5)
    for e in range(EXPERTS):
        gathered(e)
        first_product(e, acts, choice, 0, PADDED)
    for half in range(2):
        swap_cores(0, half)
    for half in range(2):
        sum_group(0, half)
    refit(4)
    refit(5)
    pass_on(4)

    a, b = iota((3 * HALF_ROWS, 4 * PACKED), 0), iota((3 * HALF_ROWS, 4 * PACKED), 1)
    to_block = jnp.where(a >= HALF_ROWS, 1, 0) + jnp.where(a >= 2 * HALF_ROWS, 1, 0)
    to_z = div_by(a - to_block * HALF_ROWS, OWN)
    row = a - to_block * HALF_ROWS - to_z * OWN
    from_z = jnp.where(b >= PACKED, 1, 0) + jnp.where(b >= 2 * PACKED, 1, 0) + jnp.where(b >= 3 * PACKED, 1, 0)
    pack = one_hot(b == from_z * PACKED + to_block * PAD + row)
    pack = jnp.where(from_z == to_z, pack, jnp.zeros_like(pack))
    unpack = pick(HALF, HALF_ROWS, PAD, OWN)
    spread = pick(4 * WIDE, HALF_ROWS, WIDE, OWN)
    ids_packed = dot(pick(ROWS, PADDED, OWN, PAD), RT[...].reshape(PADDED, 128).astype(BF16))

    def packed_choice(s, k, half):
        return ids_packed[half * HALF_ROWS : (half + 1) * HALF_ROWS, 2 * s + k : 2 * s + k + 1]

    def own_and_other(s, half):
        one, two = packed_choice(s, 0, half), packed_choice(s, 1, half)
        return jnp.where(c == 0, one, two), jnp.where(c == 0, two, one)

    def from_sums_to_parts(s):
        for half in range(2):
            hidden_units(s, half)
        if s == 0:
            gathered(4)
            gathered(5)
        totals = []
        for half in range(2):
            swap_hidden(s, half)
            totals.append(second_product(HB[s, half], own_and_other(s, half)[0], None))
        for half in range(2):
            wait_bytes(HO.at[s, half], sx_r.at[7 + half, s])
            send_sums(s, half, second_product(HO[s, half], own_and_other(s, half)[1], totals[half]))

    pass_on(5)
    from_sums_to_parts(0)
    parts = []
    for half in range(2):
        parts.append(branch_part(0, half))
        share_part(half, parts[half])
    for half in range(2):
        send_home(0, half, parts[half])
    for half in range(2):
        raw = middle_rows(half)
        acts = (raw * gains[1]).astype(BF16)
        choice = [route_column(1, k)[half * HALF : (half + 1) * HALF] for k in range(2)]
        for e in range(EXPERTS):
            first_product(e, acts, choice, half * HALF, HALF)
        swap_cores(1, half)
        send_squares(1, half, raw)
    for half in range(2):
        sum_group(1, half)
    from_sums_to_parts(1)
    store_home(0)
    for half in range(2):
        send_home(1, half, branch_part(1, half))
    store_home(1)

    for b in range(BATCHES):
        for way in range(2):
            wait_bytes(RA.at[b, way], sa_s.at[b, way])
            wait_bytes(RR.at[b, way], sr_s.at[b, way])
            where = pieces(b)
            pltpu.make_async_copy((N1, N2)[way].at[where], (new1, new2)[way].at[where], out_sem.at[b, way]).wait()
        for p in range(2):
            wait_bytes(W.at[b, p, 0, 0:3], ag_s.at[b, 0, p])
            wait_bytes(W.at[b, p, 0:3], ag_s.at[b, 1, p])
    wait_bytes(XS.at[0:7], sx_s.at[0, 0])
    wait_bytes(RT.at[0:7], st_s.at[0])
    for half in range(2):
        wait_bytes(BR.at[half, 0:3], sx_s.at[11, half])
    for s in range(2):
        for half in range(2):
            wait_bytes(SQR.at[s, half, 0:7], st_s.at[1 + 2 * s + half])
            wait_bytes(CR.at[s, half], sx_s.at[1 + half, s])
            wait_bytes(ZR.at[s, half, 0:3], sx_s.at[3 + half, s])
            wait_bytes(HB.at[s, half, 0:3], sx_s.at[5 + half, s])
            wait_bytes(HO.at[s, half], sx_s.at[7 + half, s])
            wait_bytes(YR.at[s, half, 0:3], sx_s.at[9 + half, s])
        wait_bytes(OR.at[s, 0:7], sx_s.at[12, s])


def shards(grad_stack, master_weight, moment_one, moment_two, decode_rows, norm_gain, route_ids, route_weights):
    dma = pltpu.SemaphoreType.DMA
    vmem = pltpu.VMEM
    scratch = [
        vmem((EXPERTS, 3, SLICE, 4 * HID), BF16),
        vmem((3, EXPERTS, 3, SLICE, HID), F32),
        vmem((EXPERTS, 3, SLICE, HID), F32),
        vmem((EXPERTS, 3, SLICE, HID), F32),
        vmem((BATCHES, 2, 4, 4, SLICE, HID), BF16),
        vmem((BATCHES, 2, 2, 16, HID), BF16),
        vmem((BATCHES, 2, 2, 16, HID), BF16),
        vmem((BATCHES, 2, 2, SLICE, HID), BF16),
        vmem((OWN, D), BF16),
        vmem((2, D), BF16),
        vmem((2, 2, OWN), jnp.int32),
        vmem((2, 2, OWN), F32),
        vmem((WIDE, D), BF16),
        vmem((GROUP, 4 * OWN, SEG), BF16),
        vmem((GROUP, 4 * OWN, SEG), BF16),
        vmem((GROUP, PAD, 128), F32),
        vmem((2, 2, PADDED, HID), F32),
        vmem((2, 2, 2, 2, HALF, HID), BF16),
        vmem((2, 2, 2, HALF, HID), BF16),
        vmem((2, 2, 4, BOTH, HID), BF16),
        vmem((2, 2, 4, BOTH, HID), BF16),
        vmem((2, 2, 4, 8, 128), F32),
        vmem((2, 2, GROUP, 8, 128), F32),
        vmem((2, 2, 4, PACKED, 128), BF16),
        vmem((2, 2, 4, PACKED, 128), BF16),
        vmem((2, 2, 4, HALF_ROWS, SEG), BF16),
        vmem((2, 2, 4, HALF_ROWS, SEG), BF16),
        vmem((2, 4, HALF_ROWS, SEG), BF16),
        vmem((2, GROUP, WIDE, SEG), BF16),
        vmem((2, GROUP, WIDE, SEG), BF16),
        dma((8,)),
        dma((BATCHES, 2)),
        dma((BATCHES, 2)),
        dma((BATCHES, 2)),
        dma((BATCHES, 2)),
        dma((BATCHES, 2)),
        dma((BATCHES, 2, 2)),
        dma((BATCHES, 2, 2)),
        dma((13, 2)),
        dma((13, 2)),
        dma((5,)),
        dma((5,)),
    ]
    in_vmem = pl.BlockSpec(memory_space=pltpu.VMEM)
    in_hbm = pl.BlockSpec(memory_space=pltpu.HBM)
    return pl.pallas_call(
        kernel,
        out_shape=(
            jax.ShapeDtypeStruct(moment_one.shape, F32),
            jax.ShapeDtypeStruct(moment_two.shape, F32),
            jax.ShapeDtypeStruct((2, OWN, D // 4), BF16),
        ),
        in_specs=[in_hbm] * 8,
        out_specs=(in_hbm, in_hbm, in_vmem),
        scratch_shapes=scratch,
        compiler_params=pltpu.CompilerParams(
            collective_id=0, has_side_effects=True, vmem_limit_bytes=62 * 1024 * 1024
        ),
        name="refit_and_decode",
    )(
        grad_stack,
        master_weight,
        moment_one,
        moment_two,
        decode_rows,
        norm_gain,
        route_ids.transpose(0, 2, 1),
        route_weights.transpose(0, 2, 1),
    )


def solution(mesh):
    return jax.shard_map(
        shards,
        mesh=mesh,
        in_specs=(
            P("rep", None, None, "shard", None),
            P(None, None, "shard", "rep"),
            P(None, None, "shard", "rep"),
            P(None, None, "shard", "rep"),
            P("shard", None),
            P(),
            P(None, "shard", None),
            P(None, "shard", None),
        ),
        out_specs=(
            P(None, None, "shard", "rep"),
            P(None, None, "shard", "rep"),
            P(None, "shard", "rep"),
        ),
        check_vma=False,
    )
```

time: 158 us -> 142 us (0.90)
  Pallas kernels: 147 us -> 137 us
  local copies, waits for them, and re-layouts: 10 us -> 4.41 us
    pallas_call x1, Pallas kernels: 147 us -> 137 us  [shards(): pl.pallas_call(kernel, out_shape=(jax.ShapeDtypeStruct(moment_one.shape,...]
    unnamed x16 -> x4, local copies, waits for them, and re-layouts: 9.29 us -> 2.74 us
where the time goes in v2:
time: 142 us
  Pallas kernels  137 us (96%)
  local copies, waits for them, and re-layouts  4.41 us (3%)
    pallas_call x1, Pallas kernels, shards(): pl.pallas_call(kernel, out_shape=(jax.ShapeDtypeStruct(moment_one.shape,...  137 us

profile of v2, /device:TPU:1, one launch (start us, length us, event | category | flops | bytes accessed | tf_op | source)
XLA Modules:
  0.0 141.8 jit_solution(5553082538358909048)
XLA Ops:
  0.6 136.7 %refit_and_decode.1 = (f32[4,3,32,384]{3,2,1,0:T(8,128)}, f32[4,3,32,384]{3,2,1,0:T(8,128)}, bf16[2,20,1024]{2,1,0:T(8,128)(2,1)}) custom-call(bf16[1,4,3,32,1536]{4,3,2,1,0:T(8,128)(2,1)} %grads.1, f32[4,3,32,384]{3,2,1,0:T(8,128)} %master.1, f32[4,3,32,384]{3,2,1,0:T(8,128)} %mom1.1, f32[4,3,32,384]{3,2,1,0:T(8,128)} %mom2.1, bf16[20,4096]{1,0:T(8,128)(2,1)} %rows.1, ...), custom_call_target="tpu_custom_call" | custom-call | tf_op jit(solution)/shard_map/refit_and_decode/pallas_call | solution.py:611
  137.4 0.0 copy-start
  137.4 1.7 %copy.11 = bf16[2,20,1024]{2,0,1:T(2,128)(2,1)} copy(bf16[2,20,1024]{2,1,0:T(8,128)(2,1)} %get-tuple-element.5) | data formatting | bytes 163840 | tf_op jit(solution)/shard_map/refit_and_decode/pallas_call | solution.py:611
  139.0 1.9 %copy.14 = f32[4,3,32,384]{3,2,1,0:T(8,128)} copy(f32[4,3,32,384]{3,2,1,0:T(8,128)} %get-tuple-element.9) | data formatting | bytes 1179648
  141.0 0.0 copy-done
  141.0 0.8 copy.15
Async XLA Ops:
  137.4 3.6 %copy-start = (f32[4,3,32,384]{3,2,1,0:T(8,128)S(1)}, f32[4,3,32,384]{3,2,1,0:T(8,128)}, u32[]{:S(2)}) copy-start(f32[4,3,32,384]{3,2,1,0:T(8,128)} %get-tuple-element.10) | copy-start | bytes 1769476

commit v3 on v2

--- a/solution.py
+++ b/solution.py
@@ -94,6 +94,8 @@
     TB,
     ZR,
     SQS,
+    SQC,
+    SQT,
     SQR,
     HB,
     HO,
@@ -320,10 +322,8 @@
             part = squares[zz * PAD : (zz + 1) * PAD]
             line = jnp.sum(jnp.where(same, part, 0.0), axis=0, keepdims=True)
             SQS[s, half, zz] = jnp.broadcast_to(line, (8, 128))
-        SQR[s, half, t] = SQS[s, half, z]
-        for (zz, _), peer in zip(group_steps, group_peers):
-            src = SQS.at[s, half, zz]
-            send(src, SQR.at[s, half, t], st_s.at[1 + 2 * s + half], st_r.at[1 + 2 * s + half], peer)
+        n = 1 + 2 * s + half
+        send(SQS.at[s, half], SQC.at[s, half], st_s.at[n], st_r.at[n], core_peer)
 
     def first_product(e, activations, choice, first, count):
         gate = dot(activations, W[e, 0].reshape(LOCAL, HID))
@@ -343,6 +343,12 @@
         send(PB.at[s, half, 1 - c], CR.at[s, half], sx_s.at[1 + half, s], sx_r.at[1 + half, s], core_peer)
 
     def sum_group(s, half):
+        wait_bytes(SQC.at[s, half], st_r.at[1 + 2 * s + half])
+        SQT[s, half] = SQS[s, half] + SQC[s, half]
+        n = 5 + 2 * s + half
+        for zz, peer in zip(z_steps, z_peers):
+            send(SQT.at[s, half, zz], SQR.at[s, half, z], st_s.at[n], st_r.at[n], peer)
+        SQR[s, half, z] = SQT[s, half, z]
         wait_bytes(CR.at[s, half], sx_r.at[1 + half, s])
         gate = PB[s, half, c, 0].astype(F32) + CR[s, half, 0].astype(F32)
         up = PB[s, half, c, 1].astype(F32) + CR[s, half, 1].astype(F32)
@@ -354,7 +360,7 @@
         ZR[s, half, z] = TB[s, half, z]
 
     def hidden_units(s, half):
-        wait_bytes(SQR.at[s, half, 0:7], st_r.at[1 + 2 * s + half])
+        wait_bytes(SQR.at[s, half, 0:3], st_r.at[5 + 2 * s + half])
         total = jnp.sum(SQR[s, half][:, 0, :], axis=0, keepdims=True)
         scale_line = lax.rsqrt(total / float(D) + 1e-06)
         scale = jnp.sum(jnp.where(same, scale_line, 0.0), axis=1, keepdims=True)
@@ -503,13 +509,12 @@
         if s == 0:
             gathered(4)
             gathered(5)
-        totals = []
         for half in range(2):
+            own, other = own_and_other(s, half)
             swap_hidden(s, half)
-            totals.append(second_product(HB[s, half], own_and_other(s, half)[0], None))
-        for half in range(2):
+            total = second_product(HB[s, half], own, None)
             wait_bytes(HO.at[s, half], sx_r.at[7 + half, s])
-            send_sums(s, half, second_product(HO[s, half], own_and_other(s, half)[1], totals[half]))
+            send_sums(s, half, second_product(HO[s, half], other, total))
 
     pass_on(5)
     from_sums_to_parts(0)
@@ -527,7 +532,6 @@
             first_product(e, acts, choice, half * HALF, HALF)
         swap_cores(1, half)
         send_squares(1, half, raw)
-    for half in range(2):
         sum_group(1, half)
     from_sums_to_parts(1)
     store_home(0)
@@ -550,7 +554,8 @@
         wait_bytes(BR.at[half, 0:3], sx_s.at[11, half])
     for s in range(2):
         for half in range(2):
-            wait_bytes(SQR.at[s, half, 0:7], st_s.at[1 + 2 * s + half])
+            wait_bytes(SQC.at[s, half], st_s.at[1 + 2 * s + half])
+            wait_bytes(SQR.at[s, half, 0:3], st_s.at[5 + 2 * s + half])
             wait_bytes(CR.at[s, half], sx_s.at[1 + half, s])
             wait_bytes(ZR.at[s, half, 0:3], sx_s.at[3 + half, s])
             wait_bytes(HB.at[s, half, 0:3], sx_s.at[5 + half, s])
@@ -585,7 +590,9 @@
         vmem((2, 2, 4, BOTH, HID), BF16),
         vmem((2, 2, 4, BOTH, HID), BF16),
         vmem((2, 2, 4, 8, 128), F32),
-        vmem((2, 2, GROUP, 8, 128), F32),
+        vmem((2, 2, 4, 8, 128), F32),
+        vmem((2, 2, 4, 8, 128), F32),
+        vmem((2, 2, 4, 8, 128), F32),
         vmem((2, 2, 4, PACKED, 128), BF16),
         vmem((2, 2, 4, PACKED, 128), BF16),
         vmem((2, 2, 4, HALF_ROWS, SEG), BF16),
@@ -603,8 +610,8 @@
         dma((BATCHES, 2, 2)),
         dma((13, 2)),
         dma((13, 2)),
-        dma((5,)),
-        dma((5,)),
+        dma((9,)),
+        dma((9,)),
     ]
     in_vmem = pl.BlockSpec(memory_space=pltpu.VMEM)
     in_hbm = pl.BlockSpec(memory_space=pltpu.HBM)

time: 142 us -> 137 us (0.965)
  Pallas kernels: 137 us -> 132 us
    pallas_call x1, Pallas kernels: 137 us -> 132 us  [shards(): pl.pallas_call(kernel, out_shape=(jax.ShapeDtypeStruct(moment_one.shape,...]
where the time goes in v3:
time: 137 us
  Pallas kernels  132 us (96%)
  local copies, waits for them, and re-layouts  4.41 us (3%)
    pallas_call x1, Pallas kernels, shards(): pl.pallas_call(kernel, out_shape=(jax.ShapeDtypeStruct(moment_one.shape,...  132 us

profile of v3, /device:TPU:1, one launch (start us, length us, event | category | flops | bytes accessed | tf_op | source)
XLA Modules:
  0.0 136.7 jit_solution(7901260966693814915)
XLA Ops:
  0.6 131.6 %refit_and_decode.1 = (f32[4,3,32,384]{3,2,1,0:T(8,128)}, f32[4,3,32,384]{3,2,1,0:T(8,128)}, bf16[2,20,1024]{2,1,0:T(8,128)(2,1)}) custom-call(bf16[1,4,3,32,1536]{4,3,2,1,0:T(8,128)(2,1)} %grads.1, f32[4,3,32,384]{3,2,1,0:T(8,128)} %master.1, f32[4,3,32,384]{3,2,1,0:T(8,128)} %mom1.1, f32[4,3,32,384]{3,2,1,0:T(8,128)} %mom2.1, bf16[20,4096]{1,0:T(8,128)(2,1)} %rows.1, ...), custom_call_target="tpu_custom_call" | custom-call | tf_op jit(solution)/shard_map/refit_and_decode/pallas_call | solution.py:618
  132.3 0.0 copy-start
  132.3 1.7 %copy.11 = bf16[2,20,1024]{2,0,1:T(2,128)(2,1)} copy(bf16[2,20,1024]{2,1,0:T(8,128)(2,1)} %get-tuple-element.5) | data formatting | bytes 163840 | tf_op jit(solution)/shard_map/refit_and_decode/pallas_call | solution.py:618
  133.9 1.9 %copy.14 = f32[4,3,32,384]{3,2,1,0:T(8,128)} copy(f32[4,3,32,384]{3,2,1,0:T(8,128)} %get-tuple-element.9) | data formatting | bytes 1179648
  135.9 0.0 copy-done
  135.9 0.8 copy.15
Async XLA Ops:
  132.3 3.6 %copy-start = (f32[4,3,32,384]{3,2,1,0:T(8,128)S(1)}, f32[4,3,32,384]{3,2,1,0:T(8,128)}, u32[]{:S(2)}) copy-start(f32[4,3,32,384]{3,2,1,0:T(8,128)} %get-tuple-element.10) | copy-start | bytes 1769476

commit v4 on v3

--- a/solution.py
+++ b/solution.py
@@ -131,7 +131,7 @@
     def ahead(value, by):
         return lax.rem(value + by, 4)
 
-    rep_peers = [(ahead(h, by), shard) for by in (1, 2, 3)]
+    rep_peers = [(ahead(h, by), shard) for by in (2, 1, 3)]
     x_peers = [(h, at(y, z, ahead(x, by), c)) for by in (1, 2, 3)]
     y_peers = [(h, at(ahead(y, by), z, x, c)) for by in (1, 2, 3)]
     z_steps = [ahead(z, by) for by in (1, 2, 3)]
@@ -475,15 +475,16 @@
         send_squares(0, half, raw[half * HALF : (half + 1) * HALF])
     send_summed(5)
     for e in range(EXPERTS):
+        if e == 3:
+            refit(4)
         gathered(e)
         first_product(e, acts, choice, 0, PADDED)
     for half in range(2):
         swap_cores(0, half)
+    pass_on(4)
     for half in range(2):
         sum_group(0, half)
-    refit(4)
     refit(5)
-    pass_on(4)
 
     a, b = iota((3 * HALF_ROWS, 4 * PACKED), 0), iota((3 * HALF_ROWS, 4 * PACKED), 1)
     to_block = jnp.where(a >= HALF_ROWS, 1, 0) + jnp.where(a >= 2 * HALF_ROWS, 1, 0)

time: 137 us -> 140 us (1.022)
  Pallas kernels: 132 us -> 134 us
    pallas_call x1, Pallas kernels: 132 us -> 134 us  [shards(): pl.pallas_call(kernel, out_shape=(jax.ShapeDtypeStruct(moment_one.shape,...]
where the time goes in v4:
time: 140 us; the launch traced here: 139 us
  Pallas kernels  134 us (96%)
  local copies, waits for them, and re-layouts  4.41 us (3%)
    pallas_call x1, Pallas kernels, shards(): pl.pallas_call(kernel, out_shape=(jax.ShapeDtypeStruct(moment_one.shape,...  134 us

profile of v4, /device:TPU:1, one launch (start us, length us, event | category | flops | bytes accessed | tf_op | source)
XLA Modules:
  0.0 139.4 jit_solution(2343957422072655523)
XLA Ops:
  0.6 134.4 %refit_and_decode.1 = (f32[4,3,32,384]{3,2,1,0:T(8,128)}, f32[4,3,32,384]{3,2,1,0:T(8,128)}, bf16[2,20,1024]{2,1,0:T(8,128)(2,1)}) custom-call(bf16[1,4,3,32,1536]{4,3,2,1,0:T(8,128)(2,1)} %grads.1, f32[4,3,32,384]{3,2,1,0:T(8,128)} %master.1, f32[4,3,32,384]{3,2,1,0:T(8,128)} %mom1.1, f32[4,3,32,384]{3,2,1,0:T(8,128)} %mom2.1, bf16[20,4096]{1,0:T(8,128)(2,1)} %rows.1, ...), custom_call_target="tpu_custom_call" | custom-call | tf_op jit(solution)/shard_map/refit_and_decode/pallas_call | solution.py:619
  135.0 0.0 copy-start
  135.0 1.7 %copy.11 = bf16[2,20,1024]{2,0,1:T(2,128)(2,1)} copy(bf16[2,20,1024]{2,1,0:T(8,128)(2,1)} %get-tuple-element.5) | data formatting | bytes 163840 | tf_op jit(solution)/shard_map/refit_and_decode/pallas_call | solution.py:619
  136.7 1.9 %copy.14 = f32[4,3,32,384]{3,2,1,0:T(8,128)} copy(f32[4,3,32,384]{3,2,1,0:T(8,128)} %get-tuple-element.9) | data formatting | bytes 1179648
  138.6 0.0 copy-done
  138.6 0.8 copy.15
Async XLA Ops:
  135.0 3.6 %copy-start = (f32[4,3,32,384]{3,2,1,0:T(8,128)S(1)}, f32[4,3,32,384]{3,2,1,0:T(8,128)}, u32[]{:S(2)}) copy-start(f32[4,3,32,384]{3,2,1,0:T(8,128)} %get-tuple-element.10) | copy-start | bytes 1769476

commit v5 on v4

--- a/solution.py
+++ b/solution.py
@@ -131,7 +131,7 @@
     def ahead(value, by):
         return lax.rem(value + by, 4)
 
-    rep_peers = [(ahead(h, by), shard) for by in (2, 1, 3)]
+    rep_peers = [(ahead(h, by), shard) for by in (1, 2, 3)]
     x_peers = [(h, at(y, z, ahead(x, by), c)) for by in (1, 2, 3)]
     y_peers = [(h, at(ahead(y, by), z, x, c)) for by in (1, 2, 3)]
     z_steps = [ahead(z, by) for by in (1, 2, 3)]
@@ -481,9 +481,9 @@
         first_product(e, acts, choice, 0, PADDED)
     for half in range(2):
         swap_cores(0, half)
+    for half in range(2):
+        sum_group(0, half)
     pass_on(4)
-    for half in range(2):
-        sum_group(0, half)
     refit(5)
 
     a, b = iota((3 * HALF_ROWS, 4 * PACKED), 0), iota((3 * HALF_ROWS, 4 * PACKED), 1)

time: 140 us -> 140 us (level)
  no operation moved by 1% of the time
where the time goes in v5:
time: 140 us
  Pallas kernels  135 us (96%)
  local copies, waits for them, and re-layouts  4.41 us (3%)
    pallas_call x1, Pallas kernels, shards(): pl.pallas_call(kernel, out_shape=(jax.ShapeDtypeStruct(moment_one.shape,...  135 us

profile of v5, /device:TPU:1, one launch (start us, length us, event | category | flops | bytes accessed | tf_op | source)
XLA Modules:
  0.0 139.8 jit_solution(10471130139904388923)
XLA Ops:
  0.6 134.8 %refit_and_decode.1 = (f32[4,3,32,384]{3,2,1,0:T(8,128)}, f32[4,3,32,384]{3,2,1,0:T(8,128)}, bf16[2,20,1024]{2,1,0:T(8,128)(2,1)}) custom-call(bf16[1,4,3,32,1536]{4,3,2,1,0:T(8,128)(2,1)} %grads.1, f32[4,3,32,384]{3,2,1,0:T(8,128)} %master.1, f32[4,3,32,384]{3,2,1,0:T(8,128)} %mom1.1, f32[4,3,32,384]{3,2,1,0:T(8,128)} %mom2.1, bf16[20,4096]{1,0:T(8,128)(2,1)} %rows.1, ...), custom_call_target="tpu_custom_call" | custom-call | tf_op jit(solution)/shard_map/refit_and_decode/pallas_call | solution.py:619
  135.4 0.0 copy-start
  135.4 1.7 %copy.11 = bf16[2,20,1024]{2,0,1:T(2,128)(2,1)} copy(bf16[2,20,1024]{2,1,0:T(8,128)(2,1)} %get-tuple-element.5) | data formatting | bytes 163840 | tf_op jit(solution)/shard_map/refit_and_decode/pallas_call | solution.py:619
  137.1 1.9 %copy.14 = f32[4,3,32,384]{3,2,1,0:T(8,128)} copy(f32[4,3,32,384]{3,2,1,0:T(8,128)} %get-tuple-element.9) | data formatting | bytes 1179648
  139.0 0.0 copy-done
  139.0 0.8 copy.15
Async XLA Ops:
  135.4 3.6 %copy-start = (f32[4,3,32,384]{3,2,1,0:T(8,128)S(1)}, f32[4,3,32,384]{3,2,1,0:T(8,128)}, u32[]{:S(2)}) copy-start(f32[4,3,32,384]{3,2,1,0:T(8,128)} %get-tuple-element.10) | copy-start | bytes 1769476
